TPU v7x, 32 devices: a whole 2x2x4 slice. The times are simulated.
32 devices in a mesh: dp: 4 (over z), fsdp: 8 (over y, x, core).
Axes of the slice: x: 2, y: 2, z: 4, core: 2. Of those that a mesh axis runs over, the one named last changes fastest.
Arguments:
- tokens: bfloat16 [12288, 2048], P(('dp', 'fsdp')), may hold values from -6 to 6
- lengths: int32 [32], P(('dp', 'fsdp')), may hold values from 1 to 384, 6144 in all
- cotangent: bfloat16 [12288, 2048], P(('dp', 'fsdp')), may hold values from -6 to 6
- attention_gain: bfloat16 [2048], P(('dp', 'fsdp')), may hold values from 0.099609375 to 1.8984375
- query_weight: bfloat16 [2048, 2048], P(('dp', 'fsdp')), may hold values from -0.125 to 0.125
- key_matrix: bfloat16 [2048, 1024], P(('dp', 'fsdp')), may hold values from -0.125 to 0.125
- value_matrix: bfloat16 [2048, 1024], P(('dp', 'fsdp')), may hold values from -0.125 to 0.125
- head_gate_weight: bfloat16 [2048, 16], P(('dp', 'fsdp')), may hold values from -0.125 to 0.125
- output_weight: bfloat16 [2048, 2048], P(('dp', 'fsdp')), may hold values from -2 to 2
- query_key_gain: bfloat16 [2, 128], P(None, ('dp', 'fsdp')), may hold values from 0.099609375 to 1.8984375
- feedforward_gain: bfloat16 [2048], P(('dp', 'fsdp')), may hold values from 0.099609375 to 1.8984375
- gate_weight: bfloat16 [2048, 6144], P(('dp', 'fsdp')), may hold values from -0.125 to 0.125
- up_weight: bfloat16 [2048, 6144], P(('dp', 'fsdp')), may hold values from -0.125 to 0.125
- down_weight: bfloat16 [6144, 2048], P(('dp', 'fsdp')), may hold values from -0.078125 to 0.078125
Outputs:
- layer_output: bfloat16 [12288, 2048], P(('dp', 'fsdp'))
- tokens_grad: bfloat16 [12288, 2048], P(('dp', 'fsdp'))
- attention_gain_grad: float32 [2048], P(('dp', 'fsdp'))
- query_grad: float32 [2048, 2048], P(('dp', 'fsdp'))
- key_grad: float32 [2048, 1024], P(('dp', 'fsdp'))
- value_grad: float32 [2048, 1024], P(('dp', 'fsdp'))
- head_gate_grad: float32 [2048, 16], P(('dp', 'fsdp'))
- output_grad: float32 [2048, 2048], P(('dp', 'fsdp'))
- query_key_gain_grad: float32 [2, 128], P(None, ('dp', 'fsdp'))
- feedforward_gain_grad: float32 [2048], P(('dp', 'fsdp'))
- gate_grad: float32 [2048, 6144], P(('dp', 'fsdp'))
- up_grad: float32 [2048, 6144], P(('dp', 'fsdp'))
- down_grad: float32 [6144, 2048], P(('dp', 'fsdp'))
Inputs may be any that keep to these rules, and one draw needn't show every extreme that they name: `lengths`: one length a sequence; they sum to 6144 and the longest is exactly 384.
All inputs are finite; a program needn't handle non-finite values. No bound on the sum of `lengths` on one device may be relied on, other than what follows from the above.
Results may differ from a plain program's by a relative error of at most 0.015.
Values may be sent and summed in bfloat16 or wider, within the bound.
A program may use at most 448 MiB of HBM per device.

v0:
```python
import jax
import jax.numpy as jnp
from jax import lax
from jax.sharding import PartitionSpec as P

EPSILON = 1e-06
ROPE_BASE = 1000000.0


def norm_scale(tensor, gain_vector):
    return (
        tensor
        * lax.rsqrt(jnp.mean(tensor * tensor, axis=-1, keepdims=True) + EPSILON)
        * gain_vector
    )


def rotary(tensor):
    length = tensor.shape[-3]
    half_size = tensor.shape[-1] // 2
    exponent = jnp.arange(half_size, dtype=jnp.float32) * (-2.0 / tensor.shape[-1])
    frequency = jnp.power(ROPE_BASE, exponent)
    angles = jnp.arange(length, dtype=jnp.float32)[:, None] * frequency[None, :]
    cosine = jnp.cos(angles)[:, None, :]
    sine_part = jnp.sin(angles)[:, None, :]
    first = tensor[..., :half_size]
    second = tensor[..., half_size:]
    return jnp.concatenate(
        [first * cosine - second * sine_part, second * cosine + first * sine_part], axis=-1
    )


def rotated_norm(tensor, gain_vector):
    return rotary(norm_scale(tensor, gain_vector))


def product(left, right):
    return jnp.dot(left, right, preferred_element_type=jnp.float32)


def product_nt(left, right):
    return lax.dot_general(
        left, right, (((1,), (1,)), ((), ())), preferred_element_type=jnp.float32
    )


def product_tn(left, right):
    return lax.dot_general(
        left, right, (((0,), (0,)), ((), ())), preferred_element_type=jnp.float32
    )


def causal_scores(query_rot, key_rot):
    length, head_count, head_size = query_rot.shape
    kv_count = key_rot.shape[1]
    grouped = query_rot.reshape(length, kv_count, head_count // kv_count, head_size)
    scores = jnp.einsum(
        "qkgd,skd->kgqs", grouped, key_rot, preferred_element_type=jnp.float32
    ) * head_size ** (-0.5)
    causal = lax.broadcasted_iota(jnp.int32, (length, length), 1) <= lax.broadcasted_iota(
        jnp.int32, (length, length), 0
    )
    return (jnp.where(causal, scores, -jnp.inf), grouped)


def local(
    tokens,
    lengths,
    cotangent,
    attention_gain,
    query_weight,
    key_matrix,
    value_matrix,
    head_gate_weight,
    output_weight,
    query_key_gain,
    feedforward_gain,
    gate_weight,
    up_weight,
    down_weight,
):
    attention_set = (
        lax.all_gather(attention_gain, ("dp", "fsdp"), axis=0, tiled=True),
        lax.all_gather(query_weight, ("dp", "fsdp"), axis=0, tiled=True),
        lax.all_gather(key_matrix, ("dp", "fsdp"), axis=0, tiled=True),
        lax.all_gather(value_matrix, ("dp", "fsdp"), axis=0, tiled=True),
        lax.all_gather(head_gate_weight, ("dp", "fsdp"), axis=0, tiled=True),
        lax.all_gather(output_weight, ("dp", "fsdp"), axis=0, tiled=True),
        lax.all_gather(query_key_gain, ("dp", "fsdp"), axis=1, tiled=True),
    )
    gain_one, weight_query, weight_key, weight_value, weight_head, weight_output, gain_pair = (
        attention_set
    )
    row_count = tokens.shape[0]
    head_size = gain_pair.shape[1]
    head_count = weight_query.shape[1] // head_size
    kv_count = weight_key.shape[1] // head_size
    group_size = head_count // kv_count
    score_scale = head_size ** (-0.5)
    inputs = tokens.astype(jnp.float32)
    live_rows = (lax.broadcasted_iota(jnp.int32, (row_count, 1), 0) < lengths[0]).astype(
        jnp.float32
    )
    normalized_input = norm_scale(inputs, gain_one.astype(jnp.float32)).astype(jnp.bfloat16)
    query_raw = product(normalized_input, weight_query).reshape(row_count, head_count, head_size)
    key_unrotated = product(normalized_input, weight_key).reshape(row_count, kv_count, head_size)
    value_rows = (
        product(normalized_input, weight_value)
        .astype(jnp.bfloat16)
        .reshape(row_count, kv_count, head_size)
    )
    gate_logit = product(normalized_input, weight_head)
    pair_float = gain_pair.astype(jnp.float32)
    query_rot = rotated_norm(query_raw, pair_float[0]).astype(jnp.bfloat16)
    key_rot = rotated_norm(key_unrotated, pair_float[1]).astype(jnp.bfloat16)
    masked, grouped = causal_scores(query_rot, key_rot)
    row_max = jnp.max(masked, axis=-1, keepdims=True)
    exp_terms = jnp.exp(masked - row_max)
    row_total = jnp.sum(exp_terms, axis=-1, keepdims=True)
    log_total = row_max + jnp.log(row_total)
    attention = exp_terms / row_total
    mixture = jnp.einsum(
        "kgqs,skd->qkgd",
        attention.astype(jnp.bfloat16),
        value_rows,
        preferred_element_type=jnp.float32,
    ).reshape(row_count, head_count, head_size)
    gate_value = jax.nn.sigmoid(gate_logit)
    gated = (
        (mixture * gate_value[:, :, None])
        .astype(jnp.bfloat16)
        .reshape(row_count, head_count * head_size)
    )
    hidden_state = inputs + product(gated, weight_output)
    feed_set = (
        lax.all_gather(feedforward_gain, ("dp", "fsdp"), axis=0, tiled=True),
        lax.all_gather(gate_weight, ("dp", "fsdp"), axis=0, tiled=True),
        lax.all_gather(up_weight, ("dp", "fsdp"), axis=0, tiled=True),
        lax.all_gather(down_weight, ("dp", "fsdp"), axis=0, tiled=True),
    )
    gain_two, weight_gate, weight_up, weight_down = feed_set
    normed_two = norm_scale(hidden_state, gain_two.astype(jnp.float32)).astype(jnp.bfloat16)
    gate_part = product(normed_two, weight_gate)
    up_part = product(normed_two, weight_up)
    gate_sigmoid = jax.nn.sigmoid(gate_part)
    silu_part = gate_part * gate_sigmoid
    inner = (silu_part * up_part).astype(jnp.bfloat16)
    layer_output = ((hidden_state + product(inner, weight_down)) * live_rows).astype(jnp.bfloat16)
    back_feed = (
        lax.all_gather(feedforward_gain, ("dp", "fsdp"), axis=0, tiled=True),
        lax.all_gather(gate_weight, ("dp", "fsdp"), axis=0, tiled=True),
        lax.all_gather(up_weight, ("dp", "fsdp"), axis=0, tiled=True),
        lax.all_gather(down_weight, ("dp", "fsdp"), axis=0, tiled=True),
    )
    back_gain_two, back_gate, back_up, back_down = back_feed
    upstream = cotangent.astype(jnp.float32) * live_rows
    upstream_low = upstream.astype(jnp.bfloat16)
    down_grad = product_tn(inner, upstream_low)
    inner_grad = product_nt(upstream_low, back_down)
    gate_part_back = (
        inner_grad * up_part * (gate_sigmoid + gate_part * gate_sigmoid * (1.0 - gate_sigmoid))
    ).astype(jnp.bfloat16)
    up_part_back = (inner_grad * silu_part).astype(jnp.bfloat16)
    gate_grad = product_tn(normed_two, gate_part_back)
    up_grad = product_tn(normed_two, up_part_back)
    normed_two_grad = product_nt(gate_part_back, back_gate) + product_nt(up_part_back, back_up)
    _, second_pull = jax.vjp(norm_scale, hidden_state, back_gain_two.astype(jnp.float32))
    hidden_part, feedforward_gain_grad = second_pull(normed_two_grad)
    feed_terms = (feedforward_gain_grad, gate_grad, up_grad, down_grad)
    feed_sums = (
        lax.psum_scatter(feed_terms[0], ("dp", "fsdp"), scatter_dimension=0, tiled=True),
        lax.psum_scatter(feed_terms[1], ("dp", "fsdp"), scatter_dimension=0, tiled=True),
        lax.psum_scatter(feed_terms[2], ("dp", "fsdp"), scatter_dimension=0, tiled=True),
        lax.psum_scatter(feed_terms[3], ("dp", "fsdp"), scatter_dimension=0, tiled=True),
    )
    back_attention = (
        lax.all_gather(attention_gain, ("dp", "fsdp"), axis=0, tiled=True),
        lax.all_gather(query_weight, ("dp", "fsdp"), axis=0, tiled=True),
        lax.all_gather(key_matrix, ("dp", "fsdp"), axis=0, tiled=True),
        lax.all_gather(value_matrix, ("dp", "fsdp"), axis=0, tiled=True),
        lax.all_gather(head_gate_weight, ("dp", "fsdp"), axis=0, tiled=True),
        lax.all_gather(output_weight, ("dp", "fsdp"), axis=0, tiled=True),
        lax.all_gather(query_key_gain, ("dp", "fsdp"), axis=1, tiled=True),
    )
    back_gain_one, back_query, back_key, back_value, back_head, back_output, back_pair = (
        back_attention
    )
    hidden_grad = upstream + hidden_part
    hidden_low = hidden_grad.astype(jnp.bfloat16)
    output_grad = product_tn(gated, hidden_low)
    gated_grad = product_nt(hidden_low, back_output).reshape(row_count, head_count, head_size)
    mixture_back = (gated_grad * gate_value[:, :, None]).astype(jnp.bfloat16)
    logit_back = (jnp.sum(gated_grad * mixture, axis=-1) * gate_value * (1.0 - gate_value)).astype(
        jnp.bfloat16
    )
    back_masked, _ = causal_scores(query_rot, key_rot)
    attention_again = jnp.exp(back_masked - log_total)
    mixture_grouped = mixture_back.reshape(row_count, kv_count, group_size, head_size)
    values_back = jnp.einsum(
        "kgqs,qkgd->skd",
        attention_again.astype(jnp.bfloat16),
        mixture_grouped,
        preferred_element_type=jnp.float32,
    )
    attention_grad = jnp.einsum(
        "qkgd,skd->kgqs", mixture_grouped, value_rows, preferred_element_type=jnp.float32
    )
    scores_back = (
        attention_again
        * (attention_grad - jnp.sum(attention_grad * attention_again, axis=-1, keepdims=True))
    ).astype(jnp.bfloat16)
    query_rot_grad = (
        jnp.einsum("kgqs,skd->qkgd", scores_back, key_rot, preferred_element_type=jnp.float32)
        * score_scale
    ).reshape(row_count, head_count, head_size)
    key_rot_grad = (
        jnp.einsum("kgqs,qkgd->skd", scores_back, grouped, preferred_element_type=jnp.float32)
        * score_scale
    )
    back_pair_float = back_pair.astype(jnp.float32)
    _, query_pull = jax.vjp(rotated_norm, query_raw, back_pair_float[0])
    query_chain, query_gain_back = query_pull(query_rot_grad)
    _, key_pull = jax.vjp(rotated_norm, key_unrotated, back_pair_float[1])
    key_chain, key_gain_back = key_pull(key_rot_grad)
    query_key_gain_grad = jnp.stack([query_gain_back, key_gain_back], axis=0)
    query_back = query_chain.reshape(row_count, head_count * head_size).astype(jnp.bfloat16)
    key_back = key_chain.reshape(row_count, kv_count * head_size).astype(jnp.bfloat16)
    value_back = values_back.reshape(row_count, kv_count * head_size).astype(jnp.bfloat16)
    query_grad = product_tn(normalized_input, query_back)
    key_grad = product_tn(normalized_input, key_back)
    value_grad = product_tn(normalized_input, value_back)
    head_gate_grad = product_tn(normalized_input, logit_back)
    normed_grad = (
        product_nt(query_back, back_query)
        + product_nt(key_back, back_key)
        + product_nt(value_back, back_value)
        + product_nt(logit_back, back_head)
    )
    _, first_pull = jax.vjp(norm_scale, inputs, back_gain_one.astype(jnp.float32))
    input_part, attention_gain_grad = first_pull(normed_grad)
    tokens_grad = (hidden_grad + input_part).astype(jnp.bfloat16)
    attention_terms = (
        attention_gain_grad,
        query_grad,
        key_grad,
        value_grad,
        head_gate_grad,
        output_grad,
        query_key_gain_grad,
    )
    attention_sums = (
        lax.psum_scatter(attention_terms[0], ("dp", "fsdp"), scatter_dimension=0, tiled=True),
        lax.psum_scatter(attention_terms[1], ("dp", "fsdp"), scatter_dimension=0, tiled=True),
        lax.psum_scatter(attention_terms[2], ("dp", "fsdp"), scatter_dimension=0, tiled=True),
        lax.psum_scatter(attention_terms[3], ("dp", "fsdp"), scatter_dimension=0, tiled=True),
        lax.psum_scatter(attention_terms[4], ("dp", "fsdp"), scatter_dimension=0, tiled=True),
        lax.psum_scatter(attention_terms[5], ("dp", "fsdp"), scatter_dimension=0, tiled=True),
        lax.psum_scatter(attention_terms[6], ("dp", "fsdp"), scatter_dimension=1, tiled=True),
    )
    return (
        layer_output,
        tokens_grad,
        attention_sums[0],
        attention_sums[1],
        attention_sums[2],
        attention_sums[3],
        attention_sums[4],
        attention_sums[5],
        attention_sums[6],
        feed_sums[0],
        feed_sums[1],
        feed_sums[2],
        feed_sums[3],
    )


def solution(mesh):
    placed = (
        P(("dp", "fsdp"), None),
        P(("dp", "fsdp")),
        P(("dp", "fsdp"), None),
        P(("dp", "fsdp")),
        P(("dp", "fsdp"), None),
        P(("dp", "fsdp"), None),
        P(("dp", "fsdp"), None),
        P(("dp", "fsdp"), None),
        P(("dp", "fsdp"), None),
        P(None, ("dp", "fsdp")),
        P(("dp", "fsdp")),
        P(("dp", "fsdp"), None),
        P(("dp", "fsdp"), None),
        P(("dp", "fsdp"), None),
    )
    return jax.shard_map(
        local,
        mesh=mesh,
        in_specs=placed,
        out_specs=(
            P(("dp", "fsdp"), None),
            P(("dp", "fsdp"), None),
            P(("dp", "fsdp")),
            P(("dp", "fsdp"), None),
            P(("dp", "fsdp"), None),
            P(("dp", "fsdp"), None),
            P(("dp", "fsdp"), None),
            P(("dp", "fsdp"), None),
            P(None, ("dp", "fsdp")),
            P(("dp", "fsdp")),
            P(("dp", "fsdp"), None),
            P(("dp", "fsdp"), None),
            P(("dp", "fsdp"), None),
        ),
        check_vma=False,
    )
```

profile of v0, /device:TPU:1, one launch (start us, length us, event | category | flops | bytes accessed | tf_op | source)
XLA Modules:
  0.0 2990.1 jit_solution(9106156204610619273)
XLA Ops:
  12.0 42.9 %all-gather = bf16[32,4,2]{1,2,0:T(2,128)(2,1)S(1)} all-gather(bf16[1,4,2]{1,2,0:T(2,128)(2,1)S(1)} %bitcast.202), channel_id=1, replica_groups=mesh['dp'=4,'fsdp'=8] {'dp','fsdp'}, dimensions={0}, use_global_device_ids=true | all-gather | bytes 528 | tf_op jit(solution)/shard_map/all_gather | solution.py:89
  55.7 36.7 %all-reduce.10 = (bf16[2048]{0:T(1024)(128)(2,1)S(1)}, bf16[2048]{0:T(1024)(128)(2,1)S(1)}) all-reduce(bf16[2048]{0:T(1024)(128)(2,1)S(1)} %dynamic-update-slice, bf16[2048]{0:T(1024)(128)(2,1)S(1)} %dynamic-update-slice.1), channel_id=1, replica_groups=mesh['dp'=4,'fsdp'=8] {'dp','fsdp'}, use_global_device_ids=true, to_apply=%add.4 | all-reduce | flops 4096 | bytes 16384
  92.4 41.8 %all-gather.1 = bf16[32,64,16]{1,2,0:T(8,128)(2,1)S(1)} all-gather(bf16[1,64,16]{1,2,0:T(8,128)(2,1)S(1)} %bitcast.198), channel_id=1, replica_groups=mesh['dp'=4,'fsdp'=8] {'dp','fsdp'}, dimensions={0}, use_global_device_ids=true | all-gather | bytes 67584 | tf_op jit(solution)/shard_map/all_gather | solution.py:87
  140.1 4.1 fusion.75
  145.7 1.6 copy.144
  147.3 4.1 fusion.36
  153.1 1.8 subtract_convert_fusion.1
  154.9 64.1 %all-gather.14.cloned.1.call-done = bf16[2048,2048]{1,0:T(8,128)(2,1)} async-done(((bf16[64,2048]{1,0:T(8,128)(2,1)}), bf16[2048,2048]{1,0:T(8,128)(2,1)}) %all-gather.14.cloned.1.call-update) | async-done | bytes 8388624 | tf_op jit(solution)/shard_map/all_gather | solution.py:84
  219.0 5.9 convolution_bitcast_fusion
  225.6 1.7 multiply_reduce_fusion.5
  227.3 1.6 copy.148
  231.8 2.4 multiply_multiply_fusion
  237.0 2.9 fusion.12
  240.0 2.0 fusion.3
  242.0 1.7 copy-done
  243.6 2.8 fusion.9
  246.5 1.6 copy-done.42
  248.4 49.4 %all-gather.16.cloned.1.call-done = bf16[2048,2048]{1,0:T(8,128)(2,1)} async-done(((bf16[64,2048]{1,0:T(8,128)(2,1)}), bf16[2048,2048]{1,0:T(8,128)(2,1)}) %all-gather.16.cloned.1.call-update) | async-done | bytes 8388624 | tf_op jit(solution)/shard_map/all_gather | solution.py:88
  297.8 6.0 multiply_reduce_fusion.4
  303.8 1.6 copy-done.8
  305.8 148.0 %all-gather.18.cloned.1.call-done = bf16[2048,6144]{1,0:T(8,128)(2,1)} async-done(((bf16[64,6144]{1,0:T(8,128)(2,1)}), bf16[2048,6144]{1,0:T(8,128)(2,1)}) %all-gather.18.cloned.1.call-update) | async-done | bytes 25165840 | tf_op jit(solution)/shard_map/all_gather | solution.py:137
  453.7 17.1 fusion.79
  470.8 138.6 %all-gather.20.cloned.1.call-done = bf16[2048,6144]{1,0:T(8,128)(2,1)} async-done(((bf16[64,6144]{1,0:T(8,128)(2,1)}), bf16[2048,6144]{1,0:T(8,128)(2,1)}) %all-gather.20.cloned.1.call-update) | async-done | bytes 25165840 | tf_op jit(solution)/shard_map/all_gather | solution.py:138
  609.4 16.8 fusion.80
  626.1 138.9 %all-gather.22.cloned.1.call-done = bf16[6144,2048]{1,0:T(8,128)(2,1)} async-done(((bf16[192,2048]{1,0:T(8,128)(2,1)}), bf16[6144,2048]{1,0:T(8,128)(2,1)}) %all-gather.22.cloned.1.call-update) | async-done | bytes 25165840 | tf_op jit(solution)/shard_map/all_gather | solution.py:139
  765.1 24.8 multiply_convert_fusion
  789.8 17.6 fusion.81
  807.4 19.3 multiply_reduce_fusion
  826.7 3.0 fusion.15
  829.8 8.2 fusion.21
  838.7 5.8 fusion
  844.5 11.3 fusion.2
  855.8 3.9 fusion.30
  861.1 1.9 multiply_reduce_fusion.6
  865.0 2.6 fusion.66
  867.7 5.9 fusion.70
  874.5 7.2 bitcast_convert_fusion
  881.7 5.9 fusion.68
  888.9 3.9 convolution_multiply_fusion
  893.1 2.3 copy.197
  895.4 2.3 copy.196
  897.7 3.7 multiply_add_fusion.1
  901.5 3.5 multiply_reduce_fusion.1
  907.9 5.0 fusion.16
  914.1 8.5 fusion.25
  922.7 1.8 copy-done.12
  924.5 9.5 fusion.40
  935.4 22.3 fusion.84
  957.8 22.3 fusion.85
  981.5 22.2 fusion.47
  1004.9 4.3 fusion.83
  1009.2 1.8 fusion.82
  1012.1 3.5 fusion.27
  1015.7 3.0 fusion.14
  1018.6 41.4 %all-reduce.9 = (f32[2048]{0:T(1024)S(1)}, f32[2,128]{1,0:T(2,128)S(1)}, f32[2048]{0:T(1024)S(1)}) all-reduce(f32[2048]{0:T(1024)S(1)} %get-tuple-element.19, f32[2,128]{1,0:T(2,128)S(1)} %pad_maximum_fusion.3, f32[2048]{0:T(1024)S(1)} %copy-done.74), channel_id=2, replica_groups=mesh['dp'=4,'fsdp'=8] {'dp','fsdp'}, use_global_device_ids=true, to_apply=%region_13.14.clone | all-reduce | flops 4352 | bytes 34816
  1061.8 5.0 fusion.18
  1066.8 17.1 multiply_convert_fusion.4
  1085.4 57.4 %reduce-scatter.14.cloned.1.call-done = f32[64,1024]{1,0:T(8,128)} async-done(((f32[2048,1024]{1,0:T(8,128)}), f32[64,1024]{1,0:T(8,128)}) %reduce-scatter.14.cloned.1.call-update) | async-done | bytes 262160 | tf_op jit(solution)/shard_map/reduce_scatter | solution.py:254
  1142.8 147.6 %reduce-scatter.16.cloned.1.call-done = f32[64,1024]{1,0:T(8,128)} async-done(((f32[2048,1024]{1,0:T(8,128)}), f32[64,1024]{1,0:T(8,128)}) %reduce-scatter.16.cloned.1.call-update) | async-done | bytes 262160 | tf_op jit(solution)/shard_map/reduce_scatter | solution.py:255
  1290.4 187.6 %reduce-scatter.12.cloned.1.call-done = f32[64,2048]{1,0:T(8,128)} async-done(((f32[2048,2048]{1,0:T(8,128)}), f32[64,2048]{1,0:T(8,128)}) %reduce-scatter.12.cloned.1.call-update) | async-done | bytes 524304 | tf_op jit(solution)/shard_map/reduce_scatter | solution.py:253
  1478.0 187.3 %reduce-scatter.18.cloned.1.call-done = f32[64,2048]{1,0:T(8,128)} async-done(((f32[2048,2048]{1,0:T(8,128)}), f32[64,2048]{1,0:T(8,128)}) %reduce-scatter.18.cloned.1.call-update) | async-done | bytes 524304 | tf_op jit(solution)/shard_map/reduce_scatter | solution.py:257
  1665.4 441.0 %reduce-scatter.20.cloned.1.call-done = f32[64,6144]{1,0:T(8,128)} async-done(((f32[2048,6144]{1,0:T(8,128)}), f32[64,6144]{1,0:T(8,128)}) %reduce-scatter.20.cloned.1.call-update) | async-done | bytes 1572880 | tf_op jit(solution)/shard_map/reduce_scatter | solution.py:172
  2106.4 438.5 %reduce-scatter.22.cloned.1.call-done = f32[64,6144]{1,0:T(8,128)} async-done(((f32[2048,6144]{1,0:T(8,128)}), f32[64,6144]{1,0:T(8,128)}) %reduce-scatter.22.cloned.1.call-update) | async-done | bytes 1572880 | tf_op jit(solution)/shard_map/reduce_scatter | solution.py:173
  2544.9 438.5 %reduce-scatter.24.cloned.1.call-done = f32[192,2048]{1,0:T(8,128)} async-done(((f32[6144,2048]{1,0:T(8,128)}), f32[192,2048]{1,0:T(8,128)}) %reduce-scatter.24.cloned.1.call-update) | async-done | bytes 1572880 | tf_op jit(solution)/shard_map/reduce_scatter | solution.py:174
  (260 shorter events, 39.6 us)
Async XLA Ops:
  7.2 4.8 copy-start.80
  7.2 48.0 %copy-start.82 = (bf16[64]{0:T(256)(128)(2,1)S(1)}, bf16[64]{0:T(256)(128)(2,1)}, u32[]{:S(2)}) copy-start(bf16[64]{0:T(256)(128)(2,1)} %param.17) | copy-start | bytes 388
  7.2 48.3 %copy-start.83 = (bf16[64]{0:T(256)(128)(2,1)S(1)}, bf16[64]{0:T(256)(128)(2,1)}, u32[]{:S(2)}) copy-start(bf16[64]{0:T(256)(128)(2,1)} %param.24) | copy-start | bytes 388
  7.2 85.2 %copy-start.77 = (bf16[64,16]{0,1:T(8,128)(2,1)S(1)}, bf16[64,16]{0,1:T(8,128)(2,1)}, u32[]{:S(2)}) copy-start(bf16[64,16]{0,1:T(8,128)(2,1)} %param.21) | copy-start | bytes 6148
  7.2 128.5 %copy-start.3 = (bf16[384,2048]{1,0:T(8,128)(2,1)S(1)}, bf16[384,2048]{1,0:T(8,128)(2,1)}, u32[]{:S(2)}) copy-start(bf16[384,2048]{1,0:T(8,128)(2,1)} %param.14) | copy-start | bytes 4718596
  7.2 132.8 %all-gather.12.cloned.1.call-start = ((), (), s32[]{:S(2)}) async-start(), calls=%async_computation.9 | async-start | bytes 4325376 | tf_op jit(solution)/shard_map/all_gather | solution.py:85
  8.0 139.4 %all-gather.10.cloned.1.call-start = ((), (), s32[]{:S(2)}) async-start(), calls=%async_computation.8 | async-start | bytes 4325376 | tf_op jit(solution)/shard_map/all_gather | solution.py:86
  8.7 210.3 %all-gather.14.cloned.1.call-start = ((), (), s32[]{:S(2)}) async-start(), calls=%async_computation.10 | async-start | bytes 8650752 | tf_op jit(solution)/shard_map/all_gather | solution.py:84
  9.4 288.3 %all-gather.16.cloned.1.call-start = ((), (), s32[]{:S(2)}) async-start(), calls=%async_computation.11 | async-start | bytes 8650752 | tf_op jit(solution)/shard_map/all_gather | solution.py:88
  10.0 443.7 %all-gather.18.cloned.1.call-start = ((), (), s32[]{:S(2)}) async-start(), calls=%async_computation.12 | async-start | bytes 25952256 | tf_op jit(solution)/shard_map/all_gather | solution.py:137
  10.6 598.7 %all-gather.20.cloned.1.call-start = ((), (), s32[]{:S(2)}) async-start(), calls=%async_computation.13 | async-start | bytes 25952256 | tf_op jit(solution)/shard_map/all_gather | solution.py:138
  11.2 753.9 %all-gather.22.cloned.1.call-start = ((), (), s32[]{:S(2)}) async-start(), calls=%async_computation.14 | async-start | bytes 25952256 | tf_op jit(solution)/shard_map/all_gather | solution.py:139
  11.9 1072.0 %reduce-scatter.26.cloned.1.call-start = ((), (), s32[]{:S(2)}) async-start(), calls=%async_computation.22 | async-start | bytes 1081344
  92.4 126.6 %copy-start.48 = (f32[2048]{0:T(1024)}, f32[2048]{0:T(1024)S(1)}, u32[]{:S(2)}) copy-start(f32[2048]{0:T(1024)S(1)} %convert_element_type.101) | copy-start | bytes 24580
  134.5 5.5 copy-start.52
  136.8 82.2 %copy-start.60 = (f32[384]{0:T(512)}, f32[384]{0:T(512)S(1)}, u32[]{:S(2)}) copy-start(f32[384]{0:T(512)S(1)} %fusion.57) | copy-start | bytes 4612
  138.0 688.7 %copy-start.68 = (f32[384]{0:T(512)}, f32[384]{0:T(512)S(1)}, u32[]{:S(2)}) copy-start(f32[384]{0:T(512)S(1)} %fusion.56) | copy-start | bytes 4612
  140.0 94.2 %copy-start.33 = (f32[384,64]{1,0:T(8,128)}, f32[384,64]{1,0:T(8,128)S(1)}, u32[]{:S(2)}) copy-start(f32[384,64]{1,0:T(8,128)S(1)} %get-tuple-element.41) | copy-start | bytes 294916
  140.0 94.2 %copy-start.35 = (f32[384,64]{1,0:T(8,128)}, f32[384,64]{1,0:T(8,128)S(1)}, u32[]{:S(2)}) copy-start(f32[384,64]{1,0:T(8,128)S(1)} %get-tuple-element.42) | copy-start | bytes 294916
  144.2 8.4 copy-start.15
  147.3 5.2 copy-start.62
  147.3 5.2 copy-start.75
  225.5 8.7 copy-start.1
  225.5 6.3 copy-start.72
  235.9 4.0 copy-start.24
  243.6 4.5 copy-start.57
  248.1 49.7 %copy-start.4 = (bf16[384,2048]{1,0:T(8,128)(2,1)S(1)}, bf16[384,2048]{1,0:T(8,128)(2,1)}, u32[]{:S(2)}) copy-start(bf16[384,2048]{1,0:T(8,128)(2,1)} %param.14) | copy-start | bytes 4718596
  248.4 55.4 %copy-start.17 = (bf16[384,2048]{0,1:T(8,128)(2,1)}, bf16[384,2048]{0,1:T(8,128)(2,1)S(1)}, u32[]{:S(2)}) copy-start(bf16[384,2048]{0,1:T(8,128)(2,1)S(1)} %fusion.22) | copy-start | bytes 4718596
  248.4 57.1 %copy-start.66 = (f32[2048]{0:T(1024)S(1)}, f32[2048]{0:T(1024)}, u32[]{:S(2)}) copy-start(f32[2048]{0:T(1024)} %convert_element_type.107) | copy-start | bytes 24580
  303.8 540.7 %copy-start.54 = (f32[2,8,384]{2,1,0:T(8,128)}, f32[2,8,384]{2,1,0:T(8,128)S(1)}, u32[]{:S(2)}) copy-start(f32[2,8,384]{2,1,0:T(8,128)S(1)} %log_add_fusion) | copy-start | bytes 73732
  305.8 303.6 %copy-start.18 = (bf16[384,2048]{1,0:T(8,128)(2,1)}, bf16[384,2048]{1,0:T(8,128)(2,1)S(1)}, u32[]{:S(2)}) copy-start(bf16[384,2048]{1,0:T(8,128)(2,1)S(1)} %multiply_convert_fusion.5) | copy-start | bytes 4718596
  470.8 294.3 %copy-start.30 = (bf16[384,2048]{1,0:T(8,128)(2,1)S(1)}, bf16[384,2048]{1,0:T(8,128)(2,1)}, u32[]{:S(2)}) copy-start(bf16[384,2048]{1,0:T(8,128)(2,1)} %param.16) | copy-start | bytes 4718596
  789.8 17.6 copy-start.9
  807.4 19.3 copy-start.31
  826.7 11.9 slice-start
  829.8 8.2 copy-start.11
  829.8 8.9 slice-start.1
  829.8 8.9 slice-start.2
  829.8 8.9 copy-start.40
  829.8 8.9 copy-start.64
  838.0 6.5 copy-start.41
  844.5 11.3 copy-start.25
  844.5 11.3 copy-start.27
  855.8 3.9 copy-start.34
  855.8 3.9 copy-start.36
  864.9 8.6 copy-start.46
  867.6 275.1 %reduce-scatter.14.cloned.1.call-start = ((), (), s32[]{:S(2)}) async-start(), calls=%async_computation.16 | async-start | bytes 8650752 | tf_op jit(solution)/shard_map/reduce_scatter | solution.py:254
  873.6 416.8 %reduce-scatter.16.cloned.1.call-start = ((), (), s32[]{:S(2)}) async-start(), calls=%async_computation.17 | async-start | bytes 8650752 | tf_op jit(solution)/shard_map/reduce_scatter | solution.py:255
  881.7 5.9 copy-start.50
  887.6 590.4 %reduce-scatter.12.cloned.1.call-start = ((), (), s32[]{:S(2)}) async-start(), calls=%async_computation.15 | async-start | bytes 17301504 | tf_op jit(solution)/shard_map/reduce_scatter | solution.py:253
  897.7 3.7 copy-start.2
  897.7 3.7 copy-start.44
  897.7 3.7 copy-start.73
  901.4 6.5 copy-start.45
  907.9 6.2 copy-start.6
  922.6 742.7 %reduce-scatter.18.cloned.1.call-start = ((), (), s32[]{:S(2)}) async-start(), calls=%async_computation.18 | async-start | bytes 17301504 | tf_op jit(solution)/shard_map/reduce_scatter | solution.py:257
  934.1 1172.3 %reduce-scatter.20.cloned.1.call-start = ((), (), s32[]{:S(2)}) async-start(), calls=%async_computation.19 | async-start | bytes 51904512 | tf_op jit(solution)/shard_map/reduce_scatter | solution.py:172
  957.7 1587.1 %reduce-scatter.22.cloned.1.call-start = ((), (), s32[]{:S(2)}) async-start(), calls=%async_computation.20 | async-start | bytes 51904512 | tf_op jit(solution)/shard_map/reduce_scatter | solution.py:173
  980.1 2003.2 %reduce-scatter.24.cloned.1.call-start = ((), (), s32[]{:S(2)}) async-start(), calls=%async_computation.21 | async-start | bytes 51904512 | tf_op jit(solution)/shard_map/reduce_scatter | solution.py:174
  1004.9 4.3 copy-start.47
  1004.9 4.3 copy-start.81
  1004.9 6.2 slice-start.3
  1015.6 46.1 %copy-start.71 = (f32[384]{0:T(512)S(1)}, f32[384]{0:T(512)}, u32[]{:S(2)}) copy-start(f32[384]{0:T(512)} %copy-done.70) | copy-start | bytes 4612
  1061.8 5.0 copy-start.10
  (40 other events, 77.6 us)
Sparse Core Ops, SparseCore 0:
  10.9 65.4 all-gather.11
  79.3 60.7 all-gather.9
  142.9 76.0 all-gather.13
  221.7 76.0 all-gather.15
  300.5 153.2 all-gather.17
  456.5 152.8 all-gather.19
  612.2 152.7 all-gather.21
  867.7 127.3 reduce-scatter.25
  998.1 144.5 reduce-scatter.13
  1145.6 144.7 reduce-scatter.15
  1293.4 184.6 reduce-scatter.11
  1480.8 184.4 reduce-scatter.17
  1673.5 432.8 reduce-scatter.19
  2114.4 430.4 reduce-scatter.21
  2552.9 430.4 reduce-scatter.23
where the time goes:
time: 2990 us
  waiting for transfers between devices  2440 us (82%)
  matrix products  280 us (9%)
  blocking collectives  163 us (5%)
  other arithmetic  52.8 us (2%)
  local copies, waits for them, and re-layouts  36.2 us (1%)
    reduce_scatter x1, waiting for transfers between devices, local(): lax.psum_scatter(feed_terms[1], ('dp', 'fsdp'), scatter_dimension=0, tile...  441 us
    reduce_scatter x1, waiting for transfers between devices, local(): lax.psum_scatter(feed_terms[2], ('dp', 'fsdp'), scatter_dimension=0, tile...  439 us
    reduce_scatter x1, waiting for transfers between devices, local(): lax.psum_scatter(feed_terms[3], ('dp', 'fsdp'), scatter_dimension=0, tile...  438 us
    reduce_scatter x1, waiting for transfers between devices, local(): lax.psum_scatter(attention_terms[1], ('dp', 'fsdp'), scatter_dimension=0,...  188 us
    reduce_scatter x1, waiting for transfers between devices, local(): lax.psum_scatter(attention_terms[5], ('dp', 'fsdp'), scatter_dimension=0,...  187 us
    all_gather x1, waiting for transfers between devices, local(): lax.all_gather(gate_weight, ('dp', 'fsdp'), axis=0, tiled=True)  148 us
    reduce_scatter x1, waiting for transfers between devices, local(): lax.psum_scatter(attention_terms[3], ('dp', 'fsdp'), scatter_dimension=0,...  148 us
    all_gather x1, waiting for transfers between devices, local(): lax.all_gather(down_weight, ('dp', 'fsdp'), axis=0, tiled=True)  139 us
  transfers between devices with their start and end apart: 15, of which 12 were waited for; matrix products, arithmetic and copies ran while one was open for 8% of the time, Pallas kernels for 0%

commit v1 on v0

v1 whole, which is shorter than its diff:
```python
import jax
import jax.numpy as jnp
from jax import lax
from jax.sharding import PartitionSpec as P

EPSILON = 1e-06
ROPE_BASE = 1000000.0
TEAM = 8
ALL = ("dp", "fsdp")
F32 = jnp.float32
BF16 = jnp.bfloat16


def product(left, right):
    return jnp.dot(left, right, preferred_element_type=F32)


def product_nt(left, right):
    return lax.dot_general(left, right, (((1,), (1,)), ((), ())), preferred_element_type=F32)


def product_tn(left, right):
    return lax.dot_general(left, right, (((0,), (0,)), ((), ())), preferred_element_type=F32)


def world():
    return lax.axis_size(ALL)


def member():
    return lax.axis_index(ALL) % TEAM


def teams():
    return [[first + t for t in range(TEAM)] for first in range(0, world(), TEAM)]


def lines():
    return [list(range(t, world(), TEAM)) for t in range(TEAM)]


def permute(array, pairs):
    return lax.ppermute(
        array, ALL, [(team[a], team[b]) for team in teams() for a, b in pairs]
    )


def swap(array, bits):
    return permute(array, [(i, i ^ bits) for i in range(TEAM)])


def exchange(blocks):
    if lax.axis_size("fsdp") == TEAM:
        return lax.all_to_all(blocks, "fsdp", 0, 0, tiled=True)
    return lax.all_to_all(blocks, ALL, 0, 0, tiled=True, axis_index_groups=teams())


def line_gather(shard):
    if lax.axis_size("fsdp") == TEAM:
        return lax.all_gather(shard, "dp", axis=0, tiled=True)
    return lax.all_gather(shard, ALL, axis=0, tiled=True, axis_index_groups=lines())


def line_sum(array):
    if lax.axis_size("fsdp") == TEAM:
        return lax.psum_scatter(array, "dp", scatter_dimension=0, tiled=True)
    return lax.psum_scatter(array, ALL, scatter_dimension=0, tiled=True, axis_index_groups=lines())


def team_gather(own):
    half = own.shape[0] // 2
    a1 = swap(own, 1)
    a2 = swap(own, 2)
    a4 = swap(own, 4)
    a6 = jnp.concatenate([swap(a4[:half], 2), swap(a2[half:], 4)], axis=0)
    a3 = swap(a2, 1)
    a5 = swap(a4, 1)
    a7 = swap(a6, 1)
    return [own, a1, a2, a3, a4, a5, a6, a7]


def team_sum(parts):
    half = parts[0].shape[0] // 2

    def pair(r):
        return parts[r].astype(F32) + swap(parts[r + 1].astype(BF16), 1).astype(F32)

    s6 = pair(6).astype(BF16)
    u4 = swap(s6[:half], 2).astype(F32)
    u2 = swap(s6[half:], 4).astype(F32)
    s2 = pair(2)
    s4 = pair(4)
    x_top = swap(s2[:half].astype(BF16), 2).astype(F32)
    y_low = swap(s4[half:].astype(BF16), 4).astype(F32)
    x_low = swap((s2[half:] + u2).astype(BF16), 2).astype(F32)
    y_top = swap((s4[:half] + u4).astype(BF16), 4).astype(F32)
    s0 = pair(0)
    return s0 + jnp.concatenate([x_top + y_top, x_low + y_low], axis=0)


def out_weight_in(shard, groups):
    t = member()
    if groups < TEAM:
        gathered = line_gather(shard[None])
        per = TEAM // groups
        b, z = t % groups, t // per
        result = jnp.zeros_like(gathered)
        for j in range(groups):
            perm = [(i, per * ((i % groups + j) % groups) + i // groups) for i in range(TEAM)]
            piece = lax.dynamic_index_in_dim(gathered, (b + j) % groups, 0, keepdims=True)
            piece = permute(piece, perm)
            result = lax.dynamic_update_slice_in_dim(result, piece, (z - j + groups) % groups, 0)
        return result.reshape(-1, shard.shape[1])
    full = lax.all_gather(shard, ALL, axis=0, tiled=True)
    rows = full.shape[0] // TEAM
    return lax.dynamic_slice_in_dim(full, t * rows, rows, 0)


def out_weight_back(grad, groups):
    t = member()
    if groups < TEAM:
        per = TEAM // groups
        b, z = t % groups, t // per
        grad = grad.reshape(groups, -1, grad.shape[1])
        placed = jnp.zeros_like(grad)
        for j in range(groups):
            perm = [(per * ((i % groups + j) % groups) + i // groups, i) for i in range(TEAM)]
            piece = lax.dynamic_index_in_dim(grad, (z - j + groups) % groups, 0, keepdims=True)
            piece = permute(piece, perm)
            placed = lax.dynamic_update_slice_in_dim(placed, piece, (b + j) % groups, 0)
        return line_sum(placed)[0]
    whole = jnp.zeros((grad.shape[0] * TEAM, grad.shape[1]), grad.dtype)
    whole = lax.dynamic_update_slice_in_dim(whole, grad, t * grad.shape[0], 0)
    return lax.psum_scatter(whole, ALL, scatter_dimension=0, tiled=True)


def rms_pull(value, gain, grad):
    scale = lax.rsqrt(jnp.mean(value * value, axis=-1, keepdims=True) + EPSILON)
    weighted = grad * gain
    mean = jnp.mean(weighted * value, axis=-1, keepdims=True)
    back = scale * weighted - scale * scale * scale * value * mean
    return back, jnp.sum((grad * value * scale).reshape(-1, value.shape[-1]), axis=0)


def rms(value, gain):
    return value * lax.rsqrt(jnp.mean(value * value, axis=-1, keepdims=True) + EPSILON) * gain


def rotate(u, cosine, sine):
    c = u.shape[-1] // 2
    a, b = u[..., :c], u[..., c:]
    return jnp.concatenate([a * cosine - b * sine, b * cosine + a * sine], axis=-1)


def local(
    groups,
    tokens,
    lengths,
    cotangent,
    attention_gain,
    query_weight,
    key_matrix,
    value_matrix,
    head_gate_weight,
    output_weight,
    query_key_gain,
    feedforward_gain,
    gate_weight,
    up_weight,
    down_weight,
):
    t = member()
    everyone = groups * TEAM
    rows, width = tokens.shape
    rho = query_weight.shape[0]
    phi = down_weight.shape[0]
    ff = gate_weight.shape[1]
    pair_cols = query_key_gain.shape[1]
    size = pair_cols * everyone
    heads = query_weight.shape[1] // size
    mine = heads // TEAM
    q_cols = query_weight.shape[1] // TEAM
    k_cols = key_matrix.shape[1] // TEAM
    ff_cols = ff // TEAM

    small = jnp.zeros((rho, 128), BF16)
    small = small.at[:, :heads].set(head_gate_weight)
    small = small.at[:, heads].set(attention_gain)
    small = small.at[:, heads + 1].set(feedforward_gain)
    small = small.at[0, heads + 2 : heads + 2 + 2 * pair_cols].set(query_key_gain.reshape(-1))
    small = lax.all_gather(small, ALL, axis=0)
    gain_one = small[:, :, heads].reshape(-1).astype(F32)
    gain_two = small[:, :, heads + 1].reshape(-1).astype(F32)
    gain_pair = (
        small[:, 0, heads + 2 : heads + 2 + 2 * pair_cols]
        .reshape(everyone, 2, pair_cols)
        .transpose(1, 0, 2)
        .reshape(2, size)
        .astype(F32)
    )
    weight_head = lax.dynamic_slice_in_dim(
        small[:, :, :heads].reshape(-1, heads), t * mine, mine, 1
    )

    attn = jnp.concatenate(
        [
            query_weight.reshape(rho, TEAM, q_cols),
            key_matrix.reshape(rho, TEAM, k_cols),
            value_matrix.reshape(rho, TEAM, k_cols),
        ],
        axis=2,
    ).transpose(1, 0, 2)
    attn = exchange(attn).reshape(TEAM * rho, -1)
    weight_attn = line_gather(attn)
    weight_out = out_weight_in(output_weight, groups)
    weight_down = line_gather(down_weight)

    def ff_split(w):
        return w.reshape(rho, groups, TEAM, phi).transpose(2, 0, 1, 3).reshape(TEAM, rho, ff_cols)

    feed = jnp.concatenate([ff_split(gate_weight), ff_split(up_weight)], axis=2)
    feed = exchange(feed).reshape(TEAM * rho, -1)
    weight_feed = line_gather(feed)

    team_tokens = jnp.concatenate(team_gather(tokens), axis=0)
    normed = rms(team_tokens.astype(F32), gain_one).astype(BF16)
    qkv = product(normed, weight_attn)
    gate_logit = product(normed, weight_head)
    query_raw = qkv[:, :q_cols].reshape(TEAM, rows, mine, size)
    key_raw = qkv[:, q_cols : q_cols + k_cols].reshape(TEAM, rows, 1, size)
    values = qkv[:, q_cols + k_cols :].astype(BF16).reshape(TEAM, rows, size)
    exponent = jnp.arange(size // 2, dtype=F32) * (-2.0 / size)
    frequency = jnp.power(ROPE_BASE, exponent)
    angles = jnp.arange(rows, dtype=F32)[:, None] * frequency[None, :]
    cosine = jnp.cos(angles)[:, None, :]
    sine = jnp.sin(angles)[:, None, :]
    query_rot = rotate(rms(query_raw, gain_pair[0]), cosine, sine).astype(BF16)
    key_rot = rotate(rms(key_raw, gain_pair[1]), cosine, sine).astype(BF16)[:, :, 0]
    score_scale = size ** (-0.5)
    scores = jnp.einsum("bqgd,bsd->bgqs", query_rot, key_rot, preferred_element_type=F32) * score_scale
    causal = lax.broadcasted_iota(jnp.int32, (rows, rows), 1) <= lax.broadcasted_iota(
        jnp.int32, (rows, rows), 0
    )
    masked = jnp.where(causal, scores, -jnp.inf)
    terms = jnp.exp(masked - jnp.max(masked, axis=-1, keepdims=True))
    attention = terms / jnp.sum(terms, axis=-1, keepdims=True)
    mixture = jnp.einsum(
        "bgqs,bsd->bqgd", attention.astype(BF16), values, preferred_element_type=F32
    )
    gate_value = jax.nn.sigmoid(gate_logit).reshape(TEAM, rows, mine, 1)
    gated = (mixture * gate_value).astype(BF16).reshape(TEAM * rows, q_cols)

    def blocks(array):
        return [array[r * rows : (r + 1) * rows] for r in range(TEAM)]

    inputs = tokens.astype(F32)
    hidden_state = inputs + team_sum(blocks(product(gated, weight_out).astype(BF16)))

    live_rows = (lax.broadcasted_iota(jnp.int32, (rows, 1), 0) < lengths[0]).astype(F32)
    upstream = cotangent.astype(F32) * live_rows
    team_upstream = jnp.concatenate(team_gather(upstream.astype(BF16)), axis=0)
    normed_two = rms(hidden_state, gain_two).astype(BF16)
    team_two = jnp.concatenate(team_gather(normed_two), axis=0)
    both = product(team_two, weight_feed)
    gate_part, up_part = both[:, :ff_cols], both[:, ff_cols:]
    sig = jax.nn.sigmoid(gate_part)
    silu = gate_part * sig
    inner = (silu * up_part).astype(BF16)
    feed_out = team_sum(blocks(product(inner, weight_down).astype(BF16)))
    layer_output = ((hidden_state + feed_out) * live_rows).astype(BF16)

    inner_grad = product_nt(team_upstream, weight_down)
    gate_back = (inner_grad * up_part * (sig + gate_part * sig * (1.0 - sig))).astype(BF16)
    up_back = (inner_grad * silu).astype(BF16)
    feed_back = jnp.concatenate([gate_back, up_back], axis=1)
    two_grad = team_sum(blocks(product_nt(feed_back, weight_feed).astype(BF16)))
    down_part = product_tn(inner, team_upstream).astype(BF16)
    down_grad = line_sum(down_part)
    feed_part = product_tn(team_two, feed_back).astype(BF16)
    feed_grad = line_sum(feed_part)
    feed_grad = exchange(feed_grad.reshape(TEAM, rho, 2 * ff_cols))

    def ff_join(w):
        return w.reshape(TEAM, rho, groups, phi).transpose(1, 2, 0, 3).reshape(rho, ff)

    gate_grad = ff_join(feed_grad[:, :, :ff_cols])
    up_grad = ff_join(feed_grad[:, :, ff_cols:])

    hidden_part, gain_two_grad = rms_pull(hidden_state, gain_two, two_grad)
    hidden_grad = upstream + hidden_part

    team_hidden = jnp.concatenate(team_gather(hidden_grad.astype(BF16)), axis=0)
    out_part = product_tn(gated, team_hidden).astype(BF16)
    output_grad = out_weight_back(out_part, groups)
    gated_grad = product_nt(team_hidden, weight_out).reshape(TEAM, rows, mine, size)
    mixture_back = (gated_grad * gate_value).astype(BF16)
    logit_back = (
        (jnp.sum(gated_grad * mixture, axis=-1, keepdims=True) * gate_value * (1.0 - gate_value))
        .astype(BF16)
        .reshape(TEAM * rows, mine)
    )
    values_back = jnp.einsum(
        "bgqs,bqgd->bsd", attention.astype(BF16), mixture_back, preferred_element_type=F32
    )
    attention_grad = jnp.einsum("bqgd,bsd->bgqs", mixture_back, values, preferred_element_type=F32)
    scores_back = (
        attention
        * (attention_grad - jnp.sum(attention_grad * attention, axis=-1, keepdims=True))
    ).astype(BF16)
    query_rot_grad = (
        jnp.einsum("bgqs,bsd->bqgd", scores_back, key_rot, preferred_element_type=F32) * score_scale
    )
    key_rot_grad = (
        jnp.einsum("bgqs,bqgd->bsd", scores_back, query_rot, preferred_element_type=F32)
        * score_scale
    )[:, :, None]
    query_chain, query_gain_back = rms_pull(
        query_raw, gain_pair[0], rotate(query_rot_grad, cosine, -sine)
    )
    key_chain, key_gain_back = rms_pull(key_raw, gain_pair[1], rotate(key_rot_grad, cosine, -sine))
    attn_back = jnp.concatenate(
        [
            query_chain.reshape(TEAM * rows, q_cols).astype(BF16),
            key_chain.reshape(TEAM * rows, k_cols).astype(BF16),
            values_back.reshape(TEAM * rows, k_cols).astype(BF16),
        ],
        axis=1,
    )
    normed_part = product_nt(attn_back, weight_attn) + product_nt(logit_back, weight_head)
    normed_grad = team_sum(blocks(normed_part.astype(BF16)))
    input_part, gain_one_grad = rms_pull(inputs, gain_one, normed_grad)
    tokens_grad = (hidden_grad + input_part).astype(BF16)
    attn_part = product_tn(normed, attn_back).astype(BF16)
    attn_grad = line_sum(attn_part)
    attn_grad = exchange(attn_grad.reshape(TEAM, rho, -1)).transpose(1, 0, 2)
    head_part = product_tn(normed, logit_back)

    head_full = lax.dynamic_update_slice_in_dim(
        jnp.zeros((width, heads), F32), head_part, t * mine, 1
    )
    pair_grad = jnp.stack([query_gain_back, key_gain_back], axis=0)
    packed = jnp.concatenate(
        [
            head_full.reshape(everyone, rho * heads),
            gain_one_grad.reshape(everyone, rho),
            gain_two_grad.reshape(everyone, rho),
            pair_grad.reshape(2, everyone, pair_cols).transpose(1, 0, 2).reshape(everyone, -1),
        ],
        axis=1,
    )
    packed = lax.psum_scatter(packed, ALL, scatter_dimension=0, tiled=True)[0]
    head_gate_grad = packed[: rho * heads].reshape(rho, heads)
    rest = packed[rho * heads :]
    return (
        layer_output,
        tokens_grad,
        rest[:rho],
        attn_grad[:, :, :q_cols].reshape(rho, -1).astype(F32),
        attn_grad[:, :, q_cols : q_cols + k_cols].reshape(rho, -1).astype(F32),
        attn_grad[:, :, q_cols + k_cols :].reshape(rho, -1).astype(F32),
        head_gate_grad,
        output_grad.astype(F32),
        rest[2 * rho :].reshape(2, pair_cols),
        rest[rho : 2 * rho],
        gate_grad.astype(F32),
        up_grad.astype(F32),
        down_grad.astype(F32),
    )


def solution(mesh):
    groups = mesh.size // TEAM
    rows, vector, columns = P(ALL, None), P(ALL), P(None, ALL)

    def step(*args):
        return local(groups, *args)

    return jax.shard_map(
        step,
        mesh=mesh,
        in_specs=(
            rows, vector, rows, vector, rows, rows, rows, rows, rows, columns, vector, rows, rows, rows,
        ),
        out_specs=(
            rows, rows, vector, rows, rows, rows, rows, rows, columns, vector, rows, rows, rows,
        ),
        check_vma=False,
    )
```

time: 2990 us -> 1210 us (0.40)
  waiting for transfers between devices: 2440 us -> 380 us
  local copies, waits for them, and re-layouts: 36.2 us -> 217 us
  other arithmetic: 52.8 us -> 157 us
  starting transfers between devices: 1.38 us -> 105 us
  blocking collectives: 163 us -> 73.5 us
  matrix products: 280 us -> 244 us
    reduce_scatter x7 -> x4, waiting for transfers between devices: 1900 us -> 7.58 us  [line_sum(): return lax.psum_scatter(array, 'dp', scatter_dimension=0, tiled=True)]
    all_gather x7 -> x4, waiting for transfers between devices: 539 us -> 0.02 us  [line_gather(): return lax.all_gather(shard, 'dp', axis=0, tiled=True)]
    ppermute x0 -> x80, waiting for transfers between devices: none -> 249 us  [permute(): lax.ppermute(array, ALL, [(team[a], team[b]) for team in teams() for a, b...]
    unnamed x16 -> x10, waiting for transfers between devices: 4.47 us -> 121 us
    ppermute x0 -> x80, starting transfers between devices: none -> 91 us  [permute(): lax.ppermute(array, ALL, [(team[a], team[b]) for team in teams() for a, b...]
    unnamed x2 -> x0, blocking collectives: 78 us -> none
    convert_element_type x10 -> x23, other arithmetic: 24.6 us -> 78.6 us  [the longest x4 24.7 us: team_sum(): s6 = pair(6).astype(BF16)]
    unnamed x192 -> x258, local copies, waits for them, and re-layouts: 26.9 us -> 73.7 us
  transfers between devices with their start and end apart: 15 -> 92, of which waited for: 12 -> 29; matrix products, arithmetic and copies ran while one was open for 8% -> 45% of each run, Pallas kernels for 0% -> 0%
where the time goes in v1:
time: 1210 us; the launch traced here: 1190 us
  waiting for transfers between devices  380 us (31%)
  matrix products  244 us (20%)
  local copies, waits for them, and re-layouts  217 us (18%)
  other arithmetic  157 us (13%)
  starting transfers between devices  105 us (9%)
  blocking collectives  73.5 us (6%)
  between operations  16.7 us (1%)
    ppermute x80, waiting for transfers between devices, permute(): lax.ppermute(array, ALL, [(team[a], team[b]) for team in teams() for a, b...  249 us
    unnamed x10, waiting for transfers between devices  121 us
    ppermute x80, starting transfers between devices, permute(): lax.ppermute(array, ALL, [(team[a], team[b]) for team in teams() for a, b...  91 us
    dot_general x5, matrix products, product_nt(): lax.dot_general(left, right, (((1,), (1,)), ((), ())), preferred_element_...  81.5 us
    unnamed x258, local copies, waits for them, and re-layouts  73.7 us
    dot_general x5, matrix products, product_tn(): lax.dot_general(left, right, (((0,), (0,)), ((), ())), preferred_element_...  67.8 us
    all_gather x1, blocking collectives, local(): small = lax.all_gather(small, ALL, axis=0)  59.9 us
    dot_general x5, matrix products, product(): return jnp.dot(left, right, preferred_element_type=F32)  57 us
  transfers between devices with their start and end apart: 92, of which 29 were waited for; matrix products, arithmetic and copies ran while one was open for 45% of the time, Pallas kernels for 0%

profile of v1, /device:TPU:1, one launch (start us, length us, event | category | flops | bytes accessed | tf_op | source)
XLA Modules:
  0.0 1194.5 jit_solution(3275248446517959098)
XLA Ops:
  11.1 13.5 %all_to_all.20 = bf16[8,64,512]{2,1,0:T(8,128)(2,1)} all-to-all(bf16[8,64,512]{2,1,0:T(8,128)(2,1)S(1)} %copy.252), channel_id=1, replica_groups=mesh['dp'=4,'fsdp'=8] {'fsdp'}, dimensions={0} | all-to-all | bytes 1048576 | tf_op jit(solution)/shard_map/all_to_all | solution.py:54
  40.6 4.4 all-to-all-start.1
  53.3 59.9 %all_gather.22 = bf16[32,64,128]{2,1,0:T(8,128)(2,1)S(1)} all-gather(bf16[1,64,128]{2,1,0:T(8,128)(2,1)S(1)} %copy.251), channel_id=1, replica_groups=mesh['dp'=4,'fsdp'=8] {'dp','fsdp'}, dimensions={0}, use_global_device_ids=true | all-gather | bytes 540672 | tf_op jit(solution)/shard_map/all_gather | solution.py:191
  137.5 9.6 collective-permute-done.5
  163.3 7.2 fusion.1
  170.6 11.6 fusion.3
  182.2 9.9 fusion.82
  198.0 3.9 reshape.571
  202.0 4.5 multiply_reduce_fusion.4
  224.7 9.4 fusion.80
  234.1 6.9 fusion.30
  252.2 4.5 collective-permute-done.15
  257.8 4.0 add_convert_fusion.4
  271.6 9.2 collective-permute-done.17
  282.9 37.0 %collective-permute-done.19 = bf16[192,2048]{1,0:T(8,128)(2,1)S(1)} collective-permute-done((bf16[192,2048]{1,0:T(8,128)(2,1)S(1)}, bf16[192,2048]{1,0:T(8,128)(2,1)S(1)}, u32[]{:S(2)}, u32[]{:S(2)}) %collective-permute-start.19) | collective-permute-done | bytes 786464 | tf_op jit(solution)/shard_map/ppermute | solution.py:43
  322.7 8.7 collective-permute-done.14
  333.4 4.8 collective-permute-done.18
  339.8 15.3 %collective-permute-done.21 = bf16[192,2048]{1,0:T(8,128)(2,1)} collective-permute-done((bf16[192,2048]{1,0:T(8,128)(2,1)}, bf16[192,2048]{1,0:T(8,128)(2,1)}, u32[]{:S(2)}, u32[]{:S(2)}) %collective-permute-start.21) | collective-permute-done | bytes 786464 | tf_op jit(solution)/shard_map/ppermute | solution.py:43
  367.7 4.5 collective-permute-done.46
  373.1 5.4 collective-permute-start.44
  388.8 17.1 %collective-permute-done.25 = bf16[384,2048]{1,0:T(8,128)(2,1)} collective-permute-done((bf16[384,2048]{1,0:T(8,128)(2,1)}, bf16[384,2048]{1,0:T(8,128)(2,1)}, u32[]{:S(2)}, u32[]{:S(2)}) %collective-permute-start.25) | collective-permute-done | bytes 1572896 | tf_op jit(solution)/shard_map/ppermute | solution.py:43
  418.4 4.9 collective-permute-done.27
  441.2 26.8 %fusion.83 = f32[3072,1536]{0,1:T(8,128)} fusion(bf16[3072,2048]{1,0:T(8,128)(2,1)} %constant_dynamic-update-slice_fusion.9, bf16[2048,1536]{1,0:T(8,128)(2,1)} %all-gather.8.cloned.1.call-done), kind=kOutput, calls=%fused_computation.291 | convolution fusion | flops 19327352832 | bytes 37748736 | tf_op jit(solution)/shard_map/dot_general | solution.py:15
  467.9 23.9 %multiply_convert_fusion.1 = (bf16[3072,768]{0,1:T(8,128)(2,1)}, bf16[3072,768]{0,1:T(8,128)(2,1)}, bf16[3072,768]{0,1:T(8,128)(2,1)}) fusion(f32[3072,1536]{0,1:T(8,128)} %fusion.83, bf16[3072,2048]{1,0:T(8,128)(2,1)} %constant_dynamic-update-slice_fusion.18, bf16[768,2048]{1,0:T(8,128)(2,1)} %all-gather.10.cloned.1.call-done), kind=kOutput, calls=%fused_computation.18 | convolution fusion | flops 9696706560 | bytes 48758784 | tf_op jit(solution)/shard_map/dot_general | solution.py:19
  491.8 13.2 %convolution_convert_fusion.1 = bf16[3072,2048]{1,0:T(8,128)(2,1)S(1)} fusion(bf16[3072,768]{0,1:T(8,128)(2,1)} %get-tuple-element.160, bf16[768,2048]{1,0:T(8,128)(2,1)S(1)} %copy-done.95), kind=kOutput, calls=%fused_computation.8 | convolution fusion | flops 9669967872 | bytes 20447232 | tf_op jit(solution)/shard_map/dot_general | solution.py:15
  511.5 26.2 %convolution_convert_fusion = bf16[3072,2048]{1,0:T(8,128)(2,1)} fusion(bf16[2048,1536]{1,0:T(8,128)(2,1)} %all-gather.8.cloned.1.call-done, bf16[3072,768]{0,1:T(8,128)(2,1)} %get-tuple-element.159, bf16[3072,768]{0,1:T(8,128)(2,1)} %get-tuple-element.158), kind=kOutput, calls=%fused_computation.7 | convolution fusion | flops 19352518656 | bytes 28311552 | tf_op jit(solution)/shard_map/dot_general | solution.py:19
  537.6 5.9 fusion.71
  546.4 6.7 add_convert_fusion.3
  559.4 6.5 add_convert_fusion.2
  569.3 4.1 collective-permute-done.35
  578.1 28.9 %collective-permute-done.53 = bf16[192,2048]{1,0:T(8,128)(2,1)S(1)} collective-permute-done((bf16[192,2048]{1,0:T(8,128)(2,1)S(1)}, bf16[192,2048]{1,0:T(8,128)(2,1)S(1)}, u32[]{:S(2)}, u32[]{:S(2)}) %collective-permute-start.53) | collective-permute-done | bytes 786464 | tf_op jit(solution)/shard_map/ppermute | solution.py:43
  615.3 11.3 collective-permute-done.36
  631.9 8.8 collective-permute-done.38
  644.0 16.6 %collective-permute-done.57 = bf16[192,2048]{1,0:T(8,128)(2,1)S(1)} collective-permute-done((bf16[192,2048]{1,0:T(8,128)(2,1)S(1)}, bf16[192,2048]{1,0:T(8,128)(2,1)S(1)}, u32[]{:S(2)}, u32[]{:S(2)}) %collective-permute-start.57) | collective-permute-done | bytes 786464 | tf_op jit(solution)/shard_map/ppermute | solution.py:43
  660.9 4.8 multiply_reduce_fusion
  677.0 25.8 %collective-permute-done.61 = bf16[384,2048]{1,0:T(8,128)(2,1)S(1)} collective-permute-done((bf16[384,2048]{1,0:T(8,128)(2,1)}, bf16[384,2048]{1,0:T(8,128)(2,1)S(1)}, u32[]{:S(2)}, u32[]{:S(2)}) %collective-permute-start.61) | collective-permute-done | bytes 1572896 | tf_op jit(solution)/shard_map/ppermute | solution.py:43
  707.7 4.3 collective-permute-start.60
  711.9 15.8 %convolution_convert_fusion.4 = bf16[768,2048]{1,0:T(8,128)(2,1)} fusion(bf16[3072,768]{0,1:T(8,128)(2,1)} %get-tuple-element.160, bf16[3072,2048]{1,0:T(8,128)(2,1)} %constant_dynamic-update-slice_fusion.18), kind=kOutput, calls=%fused_computation.34 | convolution fusion | flops 9665249280 | bytes 20447232 | tf_op jit(solution)/shard_map/dot_general | solution.py:23
  747.9 6.8 convolution_convert_fusion.6
  758.9 4.5 collective-permute-start.77
  765.4 6.0 fusion.31
  771.4 6.7 fusion.4
  778.2 10.6 fusion.6
  788.8 4.4 multiply_bitcast_fusion
  800.1 4.5 copy.271
  813.6 5.2 mul.787.clone
  818.9 5.2 mul.850
  824.2 4.8 fusion.23
  828.9 6.9 bitcast_convert_fusion
  850.1 11.0 convolution_convert_fusion.5
  861.2 26.8 %convolution_convert_fusion.3 = bf16[2048,1536]{1,0:T(8,128)(2,1)} fusion(bf16[3072,2048]{1,0:T(8,128)(2,1)} %constant_dynamic-update-slice_fusion.9, bf16[3072,768]{0,1:T(8,128)(2,1)} %get-tuple-element.159, bf16[3072,768]{0,1:T(8,128)(2,1)} %get-tuple-element.158), kind=kOutput, calls=%fused_computation.23 | convolution fusion | flops 19349372928 | bytes 28311552 | tf_op jit(solution)/shard_map/dot_general | solution.py:23
  889.0 10.3 fusion.54
  899.3 15.2 %add_convert_fusion = bf16[3072,2048]{1,0:T(8,128)(2,1)} fusion(f32[3072,2048]{1,0:T(8,128)} %fusion.54, bf16[2048,512]{1,0:T(8,128)(2,1)} %all-gather.6.cloned.1.call-done, bf16[3072,128]{1,0:T(8,128)(2,1)} %bitcast.268, bf16[3072,128]{1,0:T(8,128)(2,1)S(1)} %copy-done.59, bf16[3072,256]{1,0:T(8,128)(2,1)S(1)} %copy-done.52), kind=kOutput, calls=%fused_computation.6 | convolution fusion | flops 6464471040 | bytes 42991616 | tf_op jit(solution)/shard_map/dot_general | solution.py:19
  914.5 6.1 fusion.70
  929.3 7.5 add_convert_fusion.1
  940.2 7.4 fusion.81
  956.7 6.4 dynamic_update_slice.31
  977.7 7.5 collective-permute-done.68
  985.3 20.4 %collective-permute-done.72 = bf16[192,2048]{1,0:T(8,128)(2,1)} collective-permute-done((bf16[192,2048]{1,0:T(8,128)(2,1)}, bf16[192,2048]{1,0:T(8,128)(2,1)}, u32[]{:S(2)}, u32[]{:S(2)}) %collective-permute-start.72) | collective-permute-done | bytes 786464 | tf_op jit(solution)/shard_map/ppermute | solution.py:43
  1010.0 4.9 all-to-all-start.2
  1021.8 7.6 reduce-scatter.9.cloned.1.call-done
  1029.4 4.8 all-to-all-start.3
  1034.2 5.0 fusion.18
  1039.1 120.1 %all-reduce.4.cloned.1.call-done = f32[32,1160]{1,0:T(8,128)} async-done(((f32[32,1160]{1,0:T(8,128)}), f32[32,1160]{1,0:T(8,128)}) %all-reduce.4.cloned.1.call-update) | async-done | bytes 148496
  (597 shorter events, 365.3 us)
Async XLA Ops:
  7.2 112.0 %all-gather.12.cloned.1.call-start = ((), (), s32[]{:S(2)}) async-start(), calls=%async_computation.15 | async-start | bytes 1310720 | tf_op jit(solution)/shard_map/all_gather | solution.py:60
  7.9 174.3 %all-gather.6.cloned.1.call-start = ((), (), s32[]{:S(2)}) async-start(), calls=%async_computation.8 | async-start | bytes 2621440 | tf_op jit(solution)/shard_map/all_gather | solution.py:60
  24.6 102.8 %collective-permute-start.1 = (bf16[384,2048]{1,0:T(8,128)(2,1)S(1)}, bf16[384,2048]{1,0:T(8,128)(2,1)}, u32[]{:S(2)}, u32[]{:S(2)}) collective-permute-start(bf16[384,2048]{1,0:T(8,128)(2,1)S(1)} %copy-done.10), channel_id=1, source_target_pairs={{0,2},{1,3},{2,0},{3,1},{4,6},{5,7},{6,4},{7,5},{8,10},{9,11},{10,... | collective-permute-start | bytes 4718600 | tf_op jit(solution)/shard_map/ppermute | solution.py:43
  25.7 103.9 %collective-permute-start = (bf16[384,2048]{1,0:T(8,128)(2,1)S(1)}, bf16[384,2048]{1,0:T(8,128)(2,1)}, u32[]{:S(2)}, u32[]{:S(2)}) collective-permute-start(bf16[384,2048]{1,0:T(8,128)(2,1)S(1)} %copy-done.10), channel_id=1, source_target_pairs={{0,1},{1,0},{2,3},{3,2},{4,5},{5,4},{6,7},{7,6},{8,9},{9,8},{10,11... | collective-permute-start | bytes 4718600 | tf_op jit(solution)/shard_map/ppermute | solution.py:43
  26.6 99.5 %collective-permute-start.3 = (bf16[384,2048]{1,0:T(8,128)(2,1)S(1)}, bf16[384,2048]{1,0:T(8,128)(2,1)}, u32[]{:S(2)}, u32[]{:S(2)}) collective-permute-start(bf16[384,2048]{1,0:T(8,128)(2,1)S(1)} %copy-done.10), channel_id=1, source_target_pairs={{0,4},{1,5},{2,6},{3,7},{4,0},{5,1},{6,2},{7,3},{8,12},{9,13},{10,... | collective-permute-start | bytes 4718600 | tf_op jit(solution)/shard_map/ppermute | solution.py:43
  40.6 78.5 %all-to-all-start.1 = ((bf16[8,64,1536]{2,1,0:T(8,128)(2,1)}), bf16[8,64,1536]{2,1,0:T(8,128)(2,1)}, u32[]{:S(2)}, u32[]{:S(2)}) async-start(bf16[8,64,1536]{2,1,0:T(8,128)(2,1)} %pad_maximum_fusion.8), calls=%async_computation.1 | async-start | bytes 3145728 | tf_op jit(solution)/shard_map/all_to_all | solution.py:54
  45.0 396.1 %all-gather.8.cloned.1.call-start = ((), (), s32[]{:S(2)}) async-start(), calls=%async_computation.9 | async-start | bytes 7864320 | tf_op jit(solution)/shard_map/all_gather | solution.py:60
  119.1 348.8 %all-gather.10.cloned.1.call-start = ((), (), s32[]{:S(2)}) async-start(), calls=%async_computation.10 | async-start | bytes 3932160 | tf_op jit(solution)/shard_map/all_gather | solution.py:60
  127.3 19.8 %collective-permute-start.5 = (bf16[192,2048]{1,0:T(8,128)(2,1)S(1)}, bf16[192,2048]{1,0:T(8,128)(2,1)S(1)}, u32[]{:S(2)}, u32[]{:S(2)}) collective-permute-start(bf16[192,2048]{1,0:T(8,128)(2,1)S(1)} %slice.469), channel_id=1, source_target_pairs={{0,2},{1,3},{2,0},{3,1},{4,6},{5,7},{6,4},{7,5},{8,10},{9,11},{10,... | collective-permute-start | bytes 2359304 | tf_op jit(solution)/shard_map/ppermute | solution.py:43
  128.6 22.4 %collective-permute-start.6 = (bf16[192,2048]{1,0:T(8,128)(2,1)S(1)}, bf16[192,2048]{1,0:T(8,128)(2,1)S(1)}, u32[]{:S(2)}, u32[]{:S(2)}) collective-permute-start(bf16[192,2048]{1,0:T(8,128)(2,1)S(1)} %slice.470), channel_id=1, source_target_pairs={{0,4},{1,5},{2,6},{3,7},{4,0},{5,1},{6,2},{7,3},{8,12},{9,13},{10,... | collective-permute-start | bytes 2359304 | tf_op jit(solution)/shard_map/ppermute | solution.py:43
  129.6 25.0 %collective-permute-start.2 = (bf16[384,2048]{1,0:T(8,128)(2,1)}, bf16[384,2048]{1,0:T(8,128)(2,1)S(1)}, u32[]{:S(2)}, u32[]{:S(2)}) collective-permute-start(bf16[384,2048]{1,0:T(8,128)(2,1)} %collective-permute-done.1), channel_id=1, source_target_pairs={{0,1},{1,0},{2,3},{3,2},{4,5},{5,4},{6,7},{7,6},{8,9},{9,8},{10,11... | collective-permute-start | bytes 4718600 | tf_op jit(solution)/shard_map/ppermute | solution.py:43
  135.2 23.7 %collective-permute-start.4 = (bf16[384,2048]{1,0:T(8,128)(2,1)}, bf16[384,2048]{1,0:T(8,128)(2,1)S(1)}, u32[]{:S(2)}, u32[]{:S(2)}) collective-permute-start(bf16[384,2048]{1,0:T(8,128)(2,1)} %collective-permute-done.3), channel_id=1, source_target_pairs={{0,1},{1,0},{2,3},{3,2},{4,5},{5,4},{6,7},{7,6},{8,9},{9,8},{10,11... | collective-permute-start | bytes 4718600 | tf_op jit(solution)/shard_map/ppermute | solution.py:43
  265.3 56.9 %collective-permute-start.41 = (bf16[384,2048]{1,0:T(8,128)(2,1)}, bf16[384,2048]{1,0:T(8,128)(2,1)S(1)}, u32[]{:S(2)}, u32[]{:S(2)}) collective-permute-start(bf16[384,2048]{1,0:T(8,128)(2,1)} %get-tuple-element.153), channel_id=1, source_target_pairs={{0,2},{1,3},{2,0},{3,1},{4,6},{5,7},{6,4},{7,5},{8,10},{9,11},{10,... | collective-permute-start | bytes 4718600 | tf_op jit(solution)/shard_map/ppermute | solution.py:43
  266.2 56.3 %collective-permute-start.43 = (bf16[384,2048]{1,0:T(8,128)(2,1)}, bf16[384,2048]{1,0:T(8,128)(2,1)S(1)}, u32[]{:S(2)}, u32[]{:S(2)}) collective-permute-start(bf16[384,2048]{1,0:T(8,128)(2,1)} %get-tuple-element.153), channel_id=1, source_target_pairs={{0,4},{1,5},{2,6},{3,7},{4,0},{5,1},{6,2},{7,3},{8,12},{9,13},{10,... | collective-permute-start | bytes 4718600 | tf_op jit(solution)/shard_map/ppermute | solution.py:43
  268.6 51.3 %collective-permute-start.19 = (bf16[192,2048]{1,0:T(8,128)(2,1)S(1)}, bf16[192,2048]{1,0:T(8,128)(2,1)S(1)}, u32[]{:S(2)}, u32[]{:S(2)}) collective-permute-start(bf16[192,2048]{1,0:T(8,128)(2,1)S(1)} %get-tuple-element.210), channel_id=1, source_target_pairs={{0,4},{1,5},{2,6},{3,7},{4,0},{5,1},{6,2},{7,3},{8,12},{9,13},{10,... | collective-permute-start | bytes 2359304 | tf_op jit(solution)/shard_map/ppermute | solution.py:43
  268.7 91.4 %collective-permute-start.12 = (bf16[384,2048]{1,0:T(8,128)(2,1)}, bf16[384,2048]{1,0:T(8,128)(2,1)}, u32[]{:S(2)}, u32[]{:S(2)}) collective-permute-start(bf16[384,2048]{1,0:T(8,128)(2,1)} %get-tuple-element.182), channel_id=1, source_target_pairs={{0,1},{1,0},{2,3},{3,2},{4,5},{5,4},{6,7},{7,6},{8,9},{9,8},{10,11... | collective-permute-start | bytes 4718600 | tf_op jit(solution)/shard_map/ppermute | solution.py:43
  280.7 50.7 %collective-permute-start.14 = (bf16[192,2048]{1,0:T(8,128)(2,1)}, bf16[192,2048]{1,0:T(8,128)(2,1)}, u32[]{:S(2)}, u32[]{:S(2)}) collective-permute-start(bf16[192,2048]{1,0:T(8,128)(2,1)} %slice.679), channel_id=1, source_target_pairs={{0,2},{1,3},{2,0},{3,1},{4,6},{5,7},{6,4},{7,5},{8,10},{9,11},{10,... | collective-permute-start | bytes 2359304 | tf_op jit(solution)/shard_map/ppermute | solution.py:43
  322.1 32.9 %collective-permute-start.21 = (bf16[192,2048]{1,0:T(8,128)(2,1)}, bf16[192,2048]{1,0:T(8,128)(2,1)}, u32[]{:S(2)}, u32[]{:S(2)}) collective-permute-start(bf16[192,2048]{1,0:T(8,128)(2,1)} %slice.678), channel_id=1, source_target_pairs={{0,4},{1,5},{2,6},{3,7},{4,0},{5,1},{6,2},{7,3},{8,12},{9,13},{10,... | collective-permute-start | bytes 2359304 | tf_op jit(solution)/shard_map/ppermute | solution.py:43
  322.5 33.4 %collective-permute-start.20 = (bf16[192,2048]{1,0:T(8,128)(2,1)}, bf16[192,2048]{1,0:T(8,128)(2,1)}, u32[]{:S(2)}, u32[]{:S(2)}) collective-permute-start(bf16[192,2048]{1,0:T(8,128)(2,1)} %fusion.43), channel_id=1, source_target_pairs={{0,2},{1,3},{2,0},{3,1},{4,6},{5,7},{6,4},{7,5},{8,10},{9,11},{10,... | collective-permute-start | bytes 2359304 | tf_op jit(solution)/shard_map/ppermute | solution.py:43
  331.4 48.6 %collective-permute-start.40 = (bf16[384,2048]{1,0:T(8,128)(2,1)}, bf16[384,2048]{1,0:T(8,128)(2,1)}, u32[]{:S(2)}, u32[]{:S(2)}) collective-permute-start(bf16[384,2048]{1,0:T(8,128)(2,1)} %get-tuple-element.153), channel_id=1, source_target_pairs={{0,1},{1,0},{2,3},{3,2},{4,5},{5,4},{6,7},{7,6},{8,9},{9,8},{10,11... | collective-permute-start | bytes 4718600 | tf_op jit(solution)/shard_map/ppermute | solution.py:43
  338.2 28.6 %collective-permute-start.45 = (bf16[192,2048]{1,0:T(8,128)(2,1)S(1)}, bf16[192,2048]{1,0:T(8,128)(2,1)S(1)}, u32[]{:S(2)}, u32[]{:S(2)}) collective-permute-start(bf16[192,2048]{1,0:T(8,128)(2,1)S(1)} %slice.517), channel_id=1, source_target_pairs={{0,2},{1,3},{2,0},{3,1},{4,6},{5,7},{6,4},{7,5},{8,10},{9,11},{10,... | collective-permute-start | bytes 2359304 | tf_op jit(solution)/shard_map/ppermute | solution.py:43
  355.9 28.3 %collective-permute-start.42 = (bf16[384,2048]{1,0:T(8,128)(2,1)S(1)}, bf16[384,2048]{1,0:T(8,128)(2,1)}, u32[]{:S(2)}, u32[]{:S(2)}) collective-permute-start(bf16[384,2048]{1,0:T(8,128)(2,1)S(1)} %collective-permute-done.41), channel_id=1, source_target_pairs={{0,1},{1,0},{2,3},{3,2},{4,5},{5,4},{6,7},{7,6},{8,9},{9,8},{10,11... | collective-permute-start | bytes 4718600 | tf_op jit(solution)/shard_map/ppermute | solution.py:43
  366.5 39.4 %collective-permute-start.25 = (bf16[384,2048]{1,0:T(8,128)(2,1)}, bf16[384,2048]{1,0:T(8,128)(2,1)}, u32[]{:S(2)}, u32[]{:S(2)}) collective-permute-start(bf16[384,2048]{1,0:T(8,128)(2,1)} %get-tuple-element.155), channel_id=1, source_target_pairs={{0,4},{1,5},{2,6},{3,7},{4,0},{5,1},{6,2},{7,3},{8,12},{9,13},{10,... | collective-permute-start | bytes 4718600 | tf_op jit(solution)/shard_map/ppermute | solution.py:43
  366.8 40.3 %collective-permute-start.23 = (bf16[384,2048]{1,0:T(8,128)(2,1)}, bf16[384,2048]{1,0:T(8,128)(2,1)}, u32[]{:S(2)}, u32[]{:S(2)}) collective-permute-start(bf16[384,2048]{1,0:T(8,128)(2,1)} %get-tuple-element.155), channel_id=1, source_target_pairs={{0,2},{1,3},{2,0},{3,1},{4,6},{5,7},{6,4},{7,5},{8,10},{9,11},{10,... | collective-permute-start | bytes 4718600 | tf_op jit(solution)/shard_map/ppermute | solution.py:43
  373.1 35.9 %collective-permute-start.44 = (bf16[384,2048]{1,0:T(8,128)(2,1)S(1)}, bf16[384,2048]{1,0:T(8,128)(2,1)}, u32[]{:S(2)}, u32[]{:S(2)}) collective-permute-start(bf16[384,2048]{1,0:T(8,128)(2,1)S(1)} %collective-permute-done.43), channel_id=1, source_target_pairs={{0,1},{1,0},{2,3},{3,2},{4,5},{5,4},{6,7},{7,6},{8,9},{9,8},{10,11... | collective-permute-start | bytes 4718600 | tf_op jit(solution)/shard_map/ppermute | solution.py:43
  378.5 548.1 %reduce-scatter.11.cloned.1.call-start = ((), (), s32[]{:S(2)}) async-start(), calls=%async_computation.14 | async-start | bytes 3932160 | tf_op jit(solution)/shard_map/reduce_scatter | solution.py:66
  380.0 37.2 %collective-permute-start.47 = (bf16[384,2048]{1,0:T(8,128)(2,1)S(1)}, bf16[384,2048]{1,0:T(8,128)(2,1)S(1)}, u32[]{:S(2)}, u32[]{:S(2)}) collective-permute-start(bf16[384,2048]{1,0:T(8,128)(2,1)S(1)} %pad_maximum_fusion.9), channel_id=1, source_target_pairs={{0,1},{1,0},{2,3},{3,2},{4,5},{5,4},{6,7},{7,6},{8,9},{9,8},{10,11... | collective-permute-start | bytes 4718600 | tf_op jit(solution)/shard_map/ppermute | solution.py:43
  384.1 44.6 %collective-permute-start.22 = (bf16[384,2048]{1,0:T(8,128)(2,1)}, bf16[384,2048]{1,0:T(8,128)(2,1)S(1)}, u32[]{:S(2)}, u32[]{:S(2)}) collective-permute-start(bf16[384,2048]{1,0:T(8,128)(2,1)} %get-tuple-element.155), channel_id=1, source_target_pairs={{0,1},{1,0},{2,3},{3,2},{4,5},{5,4},{6,7},{7,6},{8,9},{9,8},{10,11... | collective-permute-start | bytes 4718600 | tf_op jit(solution)/shard_map/ppermute | solution.py:43
  409.0 23.7 %collective-permute-start.24 = (bf16[384,2048]{1,0:T(8,128)(2,1)}, bf16[384,2048]{1,0:T(8,128)(2,1)S(1)}, u32[]{:S(2)}, u32[]{:S(2)}) collective-permute-start(bf16[384,2048]{1,0:T(8,128)(2,1)} %collective-permute-done.23), channel_id=1, source_target_pairs={{0,1},{1,0},{2,3},{3,2},{4,5},{5,4},{6,7},{7,6},{8,9},{9,8},{10,11... | collective-permute-start | bytes 4718600 | tf_op jit(solution)/shard_map/ppermute | solution.py:43
  510.9 33.1 %collective-permute-start.31 = (bf16[384,2048]{1,0:T(8,128)(2,1)}, bf16[384,2048]{1,0:T(8,128)(2,1)S(1)}, u32[]{:S(2)}, u32[]{:S(2)}) collective-permute-start(bf16[384,2048]{1,0:T(8,128)(2,1)} %get-tuple-element.178), channel_id=1, source_target_pairs={{0,1},{1,0},{2,3},{3,2},{4,5},{5,4},{6,7},{7,6},{8,9},{9,8},{10,11... | collective-permute-start | bytes 4718600 | tf_op jit(solution)/shard_map/ppermute | solution.py:43
  511.0 33.7 %collective-permute-start.33 = (bf16[384,2048]{1,0:T(8,128)(2,1)}, bf16[384,2048]{1,0:T(8,128)(2,1)S(1)}, u32[]{:S(2)}, u32[]{:S(2)}) collective-permute-start(bf16[384,2048]{1,0:T(8,128)(2,1)} %get-tuple-element.177), channel_id=1, source_target_pairs={{0,1},{1,0},{2,3},{3,2},{4,5},{5,4},{6,7},{7,6},{8,9},{9,8},{10,11... | collective-permute-start | bytes 4718600 | tf_op jit(solution)/shard_map/ppermute | solution.py:43
  511.5 35.0 %collective-permute-start.34 = (bf16[384,2048]{1,0:T(8,128)(2,1)S(1)}, bf16[384,2048]{1,0:T(8,128)(2,1)}, u32[]{:S(2)}, u32[]{:S(2)}) collective-permute-start(bf16[384,2048]{1,0:T(8,128)(2,1)S(1)} %get-tuple-element.176), channel_id=1, source_target_pairs={{0,1},{1,0},{2,3},{3,2},{4,5},{5,4},{6,7},{7,6},{8,9},{9,8},{10,11... | collective-permute-start | bytes 4718600 | tf_op jit(solution)/shard_map/ppermute | solution.py:43
  556.8 54.6 %collective-permute-start.32 = (bf16[192,2048]{1,0:T(8,128)(2,1)}, bf16[192,2048]{1,0:T(8,128)(2,1)}, u32[]{:S(2)}, u32[]{:S(2)}) collective-permute-start(bf16[192,2048]{1,0:T(8,128)(2,1)} %slice.677), channel_id=1, source_target_pairs={{0,2},{1,3},{2,0},{3,1},{4,6},{5,7},{6,4},{7,5},{8,10},{9,11},{10,... | collective-permute-start | bytes 2359304 | tf_op jit(solution)/shard_map/ppermute | solution.py:43
  558.4 70.1 %collective-permute-start.39 = (bf16[192,2048]{1,0:T(8,128)(2,1)}, bf16[192,2048]{1,0:T(8,128)(2,1)}, u32[]{:S(2)}, u32[]{:S(2)}) collective-permute-start(bf16[192,2048]{1,0:T(8,128)(2,1)} %slice.676), channel_id=1, source_target_pairs={{0,4},{1,5},{2,6},{3,7},{4,0},{5,1},{6,2},{7,3},{8,12},{9,13},{10,... | collective-permute-start | bytes 2359304 | tf_op jit(solution)/shard_map/ppermute | solution.py:43
  567.6 39.4 %collective-permute-start.53 = (bf16[192,2048]{1,0:T(8,128)(2,1)S(1)}, bf16[192,2048]{1,0:T(8,128)(2,1)S(1)}, u32[]{:S(2)}, u32[]{:S(2)}) collective-permute-start(bf16[192,2048]{1,0:T(8,128)(2,1)S(1)} %get-tuple-element.205), channel_id=1, source_target_pairs={{0,2},{1,3},{2,0},{3,1},{4,6},{5,7},{6,4},{7,5},{8,10},{9,11},{10,... | collective-permute-start | bytes 2359304 | tf_op jit(solution)/shard_map/ppermute | solution.py:43
  573.4 57.5 %collective-permute-start.50 = (bf16[192,2048]{1,0:T(8,128)(2,1)S(1)}, bf16[192,2048]{1,0:T(8,128)(2,1)S(1)}, u32[]{:S(2)}, u32[]{:S(2)}) collective-permute-start(bf16[192,2048]{1,0:T(8,128)(2,1)S(1)} %slice.675), channel_id=1, source_target_pairs={{0,2},{1,3},{2,0},{3,1},{4,6},{5,7},{6,4},{7,5},{8,10},{9,11},{10,... | collective-permute-start | bytes 2359304 | tf_op jit(solution)/shard_map/ppermute | solution.py:43
  576.2 33.6 %collective-permute-start.55 = (bf16[192,2048]{1,0:T(8,128)(2,1)S(1)}, bf16[192,2048]{1,0:T(8,128)(2,1)S(1)}, u32[]{:S(2)}, u32[]{:S(2)}) collective-permute-start(bf16[192,2048]{1,0:T(8,128)(2,1)S(1)} %get-tuple-element.206), channel_id=1, source_target_pairs={{0,4},{1,5},{2,6},{3,7},{4,0},{5,1},{6,2},{7,3},{8,12},{9,13},{10,... | collective-permute-start | bytes 2359304 | tf_op jit(solution)/shard_map/ppermute | solution.py:43
  609.8 30.9 %collective-permute-start.38 = (bf16[192,2048]{1,0:T(8,128)(2,1)S(1)}, bf16[192,2048]{1,0:T(8,128)(2,1)S(1)}, u32[]{:S(2)}, u32[]{:S(2)}) collective-permute-start(bf16[192,2048]{1,0:T(8,128)(2,1)S(1)} %fusion.41), channel_id=1, source_target_pairs={{0,2},{1,3},{2,0},{3,1},{4,6},{5,7},{6,4},{7,5},{8,10},{9,11},{10,... | collective-permute-start | bytes 2359304 | tf_op jit(solution)/shard_map/ppermute | solution.py:43
  611.5 49.4 %collective-permute-start.30 = (bf16[384,2048]{1,0:T(8,128)(2,1)S(1)}, bf16[384,2048]{1,0:T(8,128)(2,1)S(1)}, u32[]{:S(2)}, u32[]{:S(2)}) collective-permute-start(bf16[384,2048]{1,0:T(8,128)(2,1)S(1)} %copy-done.49), channel_id=1, source_target_pairs={{0,1},{1,0},{2,3},{3,2},{4,5},{5,4},{6,7},{7,6},{8,9},{9,8},{10,11... | collective-permute-start | bytes 4718600 | tf_op jit(solution)/shard_map/ppermute | solution.py:43
  628.5 32.3 %collective-permute-start.48 = (bf16[384,2048]{1,0:T(8,128)(2,1)S(1)}, bf16[384,2048]{1,0:T(8,128)(2,1)S(1)}, u32[]{:S(2)}, u32[]{:S(2)}) collective-permute-start(bf16[384,2048]{1,0:T(8,128)(2,1)S(1)} %copy-done.50), channel_id=1, source_target_pairs={{0,1},{1,0},{2,3},{3,2},{4,5},{5,4},{6,7},{7,6},{8,9},{9,8},{10,11... | collective-permute-start | bytes 4718600 | tf_op jit(solution)/shard_map/ppermute | solution.py:43
  630.8 29.7 %collective-permute-start.57 = (bf16[192,2048]{1,0:T(8,128)(2,1)S(1)}, bf16[192,2048]{1,0:T(8,128)(2,1)S(1)}, u32[]{:S(2)}, u32[]{:S(2)}) collective-permute-start(bf16[192,2048]{1,0:T(8,128)(2,1)S(1)} %slice.674), channel_id=1, source_target_pairs={{0,4},{1,5},{2,6},{3,7},{4,0},{5,1},{6,2},{7,3},{8,12},{9,13},{10,... | collective-permute-start | bytes 2359304 | tf_op jit(solution)/shard_map/ppermute | solution.py:43
  640.7 19.9 %collective-permute-start.56 = (bf16[192,2048]{1,0:T(8,128)(2,1)S(1)}, bf16[192,2048]{1,0:T(8,128)(2,1)S(1)}, u32[]{:S(2)}, u32[]{:S(2)}) collective-permute-start(bf16[192,2048]{1,0:T(8,128)(2,1)S(1)} %fusion.39), channel_id=1, source_target_pairs={{0,2},{1,3},{2,0},{3,1},{4,6},{5,7},{6,4},{7,5},{8,10},{9,11},{10,... | collective-permute-start | bytes 2359304 | tf_op jit(solution)/shard_map/ppermute | solution.py:43
  669.5 33.3 %collective-permute-start.61 = (bf16[384,2048]{1,0:T(8,128)(2,1)}, bf16[384,2048]{1,0:T(8,128)(2,1)S(1)}, u32[]{:S(2)}, u32[]{:S(2)}) collective-permute-start(bf16[384,2048]{1,0:T(8,128)(2,1)} %get-tuple-element.150), channel_id=1, source_target_pairs={{0,4},{1,5},{2,6},{3,7},{4,0},{5,1},{6,2},{7,3},{8,12},{9,13},{10,... | collective-permute-start | bytes 4718600 | tf_op jit(solution)/shard_map/ppermute | solution.py:43
  670.0 35.1 %collective-permute-start.59 = (bf16[384,2048]{1,0:T(8,128)(2,1)}, bf16[384,2048]{1,0:T(8,128)(2,1)}, u32[]{:S(2)}, u32[]{:S(2)}) collective-permute-start(bf16[384,2048]{1,0:T(8,128)(2,1)} %get-tuple-element.150), channel_id=1, source_target_pairs={{0,2},{1,3},{2,0},{3,1},{4,6},{5,7},{6,4},{7,5},{8,10},{9,11},{10,... | collective-permute-start | bytes 4718600 | tf_op jit(solution)/shard_map/ppermute | solution.py:43
  673.5 56.4 %collective-permute-start.58 = (bf16[384,2048]{1,0:T(8,128)(2,1)}, bf16[384,2048]{1,0:T(8,128)(2,1)}, u32[]{:S(2)}, u32[]{:S(2)}) collective-permute-start(bf16[384,2048]{1,0:T(8,128)(2,1)} %get-tuple-element.150), channel_id=1, source_target_pairs={{0,1},{1,0},{2,3},{3,2},{4,5},{5,4},{6,7},{7,6},{8,9},{9,8},{10,11... | collective-permute-start | bytes 4718600 | tf_op jit(solution)/shard_map/ppermute | solution.py:43
  703.7 24.1 %collective-permute-start.63 = (bf16[192,2048]{1,0:T(8,128)(2,1)}, bf16[192,2048]{1,0:T(8,128)(2,1)}, u32[]{:S(2)}, u32[]{:S(2)}) collective-permute-start(bf16[192,2048]{1,0:T(8,128)(2,1)} %slice.533), channel_id=1, source_target_pairs={{0,2},{1,3},{2,0},{3,1},{4,6},{5,7},{6,4},{7,5},{8,10},{9,11},{10,... | collective-permute-start | bytes 2359304 | tf_op jit(solution)/shard_map/ppermute | solution.py:43
  707.2 20.6 %collective-permute-start.64 = (bf16[192,2048]{1,0:T(8,128)(2,1)}, bf16[192,2048]{1,0:T(8,128)(2,1)}, u32[]{:S(2)}, u32[]{:S(2)}) collective-permute-start(bf16[192,2048]{1,0:T(8,128)(2,1)} %slice.534), channel_id=1, source_target_pairs={{0,4},{1,5},{2,6},{3,7},{4,0},{5,1},{6,2},{7,3},{8,12},{9,13},{10,... | collective-permute-start | bytes 2359304 | tf_op jit(solution)/shard_map/ppermute | solution.py:43
  707.7 27.8 %collective-permute-start.60 = (bf16[384,2048]{1,0:T(8,128)(2,1)}, bf16[384,2048]{1,0:T(8,128)(2,1)}, u32[]{:S(2)}, u32[]{:S(2)}) collective-permute-start(bf16[384,2048]{1,0:T(8,128)(2,1)} %collective-permute-done.59), channel_id=1, source_target_pairs={{0,1},{1,0},{2,3},{3,2},{4,5},{5,4},{6,7},{7,6},{8,9},{9,8},{10,11... | collective-permute-start | bytes 4718600 | tf_op jit(solution)/shard_map/ppermute | solution.py:43
  711.9 27.5 %collective-permute-start.62 = (bf16[384,2048]{1,0:T(8,128)(2,1)S(1)}, bf16[384,2048]{1,0:T(8,128)(2,1)}, u32[]{:S(2)}, u32[]{:S(2)}) collective-permute-start(bf16[384,2048]{1,0:T(8,128)(2,1)S(1)} %collective-permute-done.61), channel_id=1, source_target_pairs={{0,1},{1,0},{2,3},{3,2},{4,5},{5,4},{6,7},{7,6},{8,9},{9,8},{10,11... | collective-permute-start | bytes 4718600 | tf_op jit(solution)/shard_map/ppermute | solution.py:43
  727.8 248.2 %reduce-scatter.7.cloned.1.call-start = ((), (), s32[]{:S(2)}) async-start(), calls=%async_computation.12 | async-start | bytes 1310720 | tf_op jit(solution)/shard_map/reduce_scatter | solution.py:66
  755.7 82.1 %collective-permute-start.76 = (bf16[1,64,2048]{2,1,0:T(8,128)(2,1)}, bf16[1,64,2048]{2,1,0:T(8,128)(2,1)}, u32[]{:S(2)}, u32[]{:S(2)}) collective-permute-start(bf16[1,64,2048]{2,1,0:T(8,128)(2,1)} %get-tuple-element.214), channel_id=1, source_target_pairs={{0,0},{2,1},{4,2},{6,3},{1,4},{3,5},{5,6},{7,7},{8,8},{10,9},{12,1... | collective-permute-start | bytes 786440 | tf_op jit(solution)/shard_map/ppermute | solution.py:43
  758.9 81.7 %collective-permute-start.77 = (bf16[1,64,2048]{2,1,0:T(8,128)(2,1)}, bf16[1,64,2048]{2,1,0:T(8,128)(2,1)}, u32[]{:S(2)}, u32[]{:S(2)}) collective-permute-start(bf16[1,64,2048]{2,1,0:T(8,128)(2,1)} %get-tuple-element.213), channel_id=1, source_target_pairs={{2,0},{4,1},{6,2},{0,3},{3,4},{5,5},{7,6},{1,7},{10,8},{12,9},{14,... | collective-permute-start | bytes 786440 | tf_op jit(solution)/shard_map/ppermute | solution.py:43
  763.3 78.9 %collective-permute-start.78 = (bf16[1,64,2048]{2,1,0:T(8,128)(2,1)}, bf16[1,64,2048]{2,1,0:T(8,128)(2,1)}, u32[]{:S(2)}, u32[]{:S(2)}) collective-permute-start(bf16[1,64,2048]{2,1,0:T(8,128)(2,1)} %get-tuple-element.212), channel_id=1, source_target_pairs={{4,0},{6,1},{0,2},{2,3},{5,4},{7,5},{1,6},{3,7},{12,8},{14,9},{8,1... | collective-permute-start | bytes 786440 | tf_op jit(solution)/shard_map/ppermute | solution.py:43
  763.4 80.5 %collective-permute-start.79 = (bf16[1,64,2048]{2,1,0:T(8,128)(2,1)}, bf16[1,64,2048]{2,1,0:T(8,128)(2,1)}, u32[]{:S(2)}, u32[]{:S(2)}) collective-permute-start(bf16[1,64,2048]{2,1,0:T(8,128)(2,1)} %get-tuple-element.211), channel_id=1, source_target_pairs={{6,0},{0,1},{2,2},{4,3},{7,4},{1,5},{3,6},{5,7},{14,8},{8,9},{10,1... | collective-permute-start | bytes 786440 | tf_op jit(solution)/shard_map/ppermute | solution.py:43
  845.6 164.4 %reduce-scatter.5.cloned.1.call-start = ((), (), s32[]{:S(2)}) async-start(), calls=%async_computation.11 | async-start | bytes 2621440 | tf_op jit(solution)/shard_map/reduce_scatter | solution.py:66
  861.1 168.3 %reduce-scatter.9.cloned.1.call-start = ((), (), s32[]{:S(2)}) async-start(), calls=%async_computation.13 | async-start | bytes 7864320 | tf_op jit(solution)/shard_map/reduce_scatter | solution.py:66
  938.1 31.8 %collective-permute-start.71 = (bf16[192,2048]{1,0:T(8,128)(2,1)}, bf16[192,2048]{1,0:T(8,128)(2,1)}, u32[]{:S(2)}, u32[]{:S(2)}) collective-permute-start(bf16[192,2048]{1,0:T(8,128)(2,1)} %get-tuple-element.202), channel_id=1, source_target_pairs={{0,2},{1,3},{2,0},{3,1},{4,6},{5,7},{6,4},{7,5},{8,10},{9,11},{10,... | collective-permute-start | bytes 2359304 | tf_op jit(solution)/shard_map/ppermute | solution.py:43
  952.5 20.5 %collective-permute-start.73 = (bf16[192,2048]{1,0:T(8,128)(2,1)}, bf16[192,2048]{1,0:T(8,128)(2,1)}, u32[]{:S(2)}, u32[]{:S(2)}) collective-permute-start(bf16[192,2048]{1,0:T(8,128)(2,1)} %get-tuple-element.203), channel_id=1, source_target_pairs={{0,4},{1,5},{2,6},{3,7},{4,0},{5,1},{6,2},{7,3},{8,12},{9,13},{10,... | collective-permute-start | bytes 2359304 | tf_op jit(solution)/shard_map/ppermute | solution.py:43
  965.0 50.0 %collective-permute-start.66 = (bf16[384,2048]{1,0:T(8,128)(2,1)}, bf16[384,2048]{1,0:T(8,128)(2,1)}, u32[]{:S(2)}, u32[]{:S(2)}) collective-permute-start(bf16[384,2048]{1,0:T(8,128)(2,1)} %get-tuple-element.161), channel_id=1, source_target_pairs={{0,1},{1,0},{2,3},{3,2},{4,5},{5,4},{6,7},{7,6},{8,9},{9,8},{10,11... | collective-permute-start | bytes 4718600 | tf_op jit(solution)/shard_map/ppermute | solution.py:43
  969.3 38.0 %collective-permute-start.75 = (bf16[192,2048]{1,0:T(8,128)(2,1)}, bf16[192,2048]{1,0:T(8,128)(2,1)}, u32[]{:S(2)}, u32[]{:S(2)}) collective-permute-start(bf16[192,2048]{1,0:T(8,128)(2,1)} %slice.672), channel_id=1, source_target_pairs={{0,4},{1,5},{2,6},{3,7},{4,0},{5,1},{6,2},{7,3},{8,12},{9,13},{10,... | collective-permute-start | bytes 2359304 | tf_op jit(solution)/shard_map/ppermute | solution.py:43
  972.1 33.6 %collective-permute-start.72 = (bf16[192,2048]{1,0:T(8,128)(2,1)}, bf16[192,2048]{1,0:T(8,128)(2,1)}, u32[]{:S(2)}, u32[]{:S(2)}) collective-permute-start(bf16[192,2048]{1,0:T(8,128)(2,1)} %fusion.38), channel_id=1, source_target_pairs={{0,4},{1,5},{2,6},{3,7},{4,0},{5,1},{6,2},{7,3},{8,12},{9,13},{10,... | collective-permute-start | bytes 2359304 | tf_op jit(solution)/shard_map/ppermute | solution.py:43
  975.2 32.1 %collective-permute-start.74 = (bf16[192,2048]{1,0:T(8,128)(2,1)}, bf16[192,2048]{1,0:T(8,128)(2,1)}, u32[]{:S(2)}, u32[]{:S(2)}) collective-permute-start(bf16[192,2048]{1,0:T(8,128)(2,1)} %fusion.37), channel_id=1, source_target_pairs={{0,2},{1,3},{2,0},{3,1},{4,6},{5,7},{6,4},{7,5},{8,10},{9,11},{10,... | collective-permute-start | bytes 2359304 | tf_op jit(solution)/shard_map/ppermute | solution.py:43
  1015.0 144.3 %all-reduce.4.cloned.1.call-start = ((), (), s32[]{:S(2)}) async-start(), calls=%async_computation.16 | async-start | bytes 327680
  1029.4 138.5 %all-to-all-start.3 = ((bf16[8,64,1536]{2,1,0:T(8,128)(2,1)}), bf16[8,64,1536]{2,1,0:T(8,128)(2,1)}, u32[]{:S(2)}, u32[]{:S(2)}) async-start(bf16[8,64,1536]{2,1,0:T(8,128)(2,1)} %bitcast.244), calls=%async_computation.6 | async-start | bytes 3145728 | tf_op jit(solution)/shard_map/all_to_all | solution.py:54
  (139 other events, 1819.3 us)
Sparse Core Ops, SparseCore 0:
  9.6 29.8 all-gather.11
  41.1 46.7 all-gather.5
  119.3 111.1 all-gather.7
  378.6 60.0 all-gather.9
  727.9 56.9 reduce-scatter.10
  845.7 25.9 reduce-scatter.6
  874.1 42.5 reduce-scatter.4
  919.0 110.3 reduce-scatter.8
  1035.5 123.7 all-reduce.3
